TPU v7x, 256 devices: a whole 4x4x8 slice. The times are simulated.
256 devices in a mesh: ta: 4 (over x_lo, core), ha: 8 (over z), wa: 8 (over x_hi, y).
Axes of the slice: x: 4 (x_hi: 2, x_lo: 2; x = x_hi * 2 + x_lo), y: 4, z: 8, core: 2. Of those that a mesh axis runs over, the one named last changes fastest.
Arguments:
- queries: bfloat16 [4, 8, 16, 1, 384, 128], P('ta', 'ha', 'wa'), may hold values from -6 to 6
- key_tiles: bfloat16 [4, 8, 16, 1, 384, 128], P('ta', 'ha', 'wa'), may hold values from -6 to 6
- value_tiles: bfloat16 [4, 8, 16, 1, 384, 128], P('ta', 'ha', 'wa'), may hold values from -6 to 6
- forward_out: bfloat16 [4, 8, 16, 1, 384, 128], P('ta', 'ha', 'wa'), may hold values from -6 to 6
- out_grad: bfloat16 [4, 8, 16, 1, 384, 128], P('ta', 'ha', 'wa'), may hold values from -96 to 96
- pattern: int32 [1, 27], replicated, may hold values 0 or 1
- tile_active: int32 [4, 8, 16], replicated, may hold values 0 or 1
Outputs:
- query_grad: bfloat16 [4, 8, 16, 1, 384, 128], P('ta', 'ha', 'wa')
- key_grad: bfloat16 [4, 8, 16, 1, 384, 128], P('ta', 'ha', 'wa')
- value_grad: bfloat16 [4, 8, 16, 1, 384, 128], P('ta', 'ha', 'wa')
All inputs are finite; a program needn't handle non-finite values.
Results may differ from a plain program's by a relative error of at most 0.0065.
Values may be sent and summed in bfloat16 or wider, within the bound.
A program may use at most 64 MiB of HBM per device.

v0:
```python
import math

import jax
import jax.numpy as jnp
import numpy as np
from jax import lax
from jax.sharding import PartitionSpec as P

side_offsets = np.array([place for place in range(27) if place != 13], np.int32)


def from_behind(x, axis, by):
    devices = lax.axis_size(axis)
    pairs = [(i, i + by) for i in range(devices) if 0 <= i + by < devices]
    return lax.ppermute(x, axis, pairs)


def with_halo(cells, sides, width):
    for axis, dim in sides:
        count = lax.axis_size(axis)
        ends = count - 1
        head = lax.slice_in_dim(cells, 0, width, axis=dim)
        tail = lax.slice_in_dim(cells, cells.shape[dim] - width, cells.shape[dim], axis=dim)
        cells = jnp.concatenate(
            [
                lax.ppermute(tail, axis, [(i, (i + 1) % count) for i in range(ends)]),
                cells,
                lax.ppermute(head, axis, [((i + 1) % count, i) for i in range(ends)]),
            ],
            axis=dim,
        )
    return cells


def as_index(value):
    return jnp.asarray(value, dtype=jnp.int32)


def block_at(extended, offset, tile_span):
    offset = as_index(offset)
    first_time = offset // 9
    first_height = offset // 3 % 3
    first_width = offset % 3
    starts = (first_time, first_height, first_width) + tuple(
        (as_index(0) for _ in range(extended.ndim - 3))
    )
    block_shape = tuple(tile_span) + tuple(extended.shape[3:])
    return lax.dynamic_slice(extended, starts, block_shape)


def allowed_mask(inside_ext, active_ext, pattern, offset, tile_span):
    offset = as_index(offset)
    inside_here = block_at(inside_ext, offset, tile_span)
    active_here = block_at(active_ext, offset, tile_span)
    chosen = lax.dynamic_index_in_dim(pattern, offset, axis=1, keepdims=False)
    listed = (chosen[None, None, None, :] == 1) & (active_here[..., None] == 1)
    return (inside_here[..., None] == 1) & ((offset == 13) | listed)


def product(form, left, right):
    return jnp.einsum(form, left, right, preferred_element_type=jnp.float32)


def tile_scores(queries, key_block, score_scale):
    return product("abceid,abcejd->abceij", queries, key_block) * score_scale


def softmax_stats(queries, key_ext, inside_ext, active_ext, pattern, tile_span, score_scale):
    centre = tile_scores(queries, block_at(key_ext, 13, tile_span), score_scale)
    running_top = jnp.max(centre, axis=-1)
    running_sum = jnp.sum(jnp.exp(centre - running_top[..., None]), axis=-1)

    def softmax_advance(carried, offset):
        old_top, old_sum = carried
        allowed = allowed_mask(inside_ext, active_ext, pattern, offset, tile_span)[..., None, None]
        scores = tile_scores(queries, block_at(key_ext, offset, tile_span), score_scale)
        masked = jnp.where(allowed, scores, -jnp.inf)
        raised_top = jnp.maximum(old_top, jnp.max(masked, axis=-1))
        new_sum = old_sum * jnp.exp(old_top - raised_top) + jnp.sum(
            jnp.exp(masked - raised_top[..., None]), axis=-1
        )
        return ((raised_top, new_sum), None)

    (running_top, running_sum), _ = lax.scan(
        softmax_advance, (running_top, running_sum), jnp.asarray(side_offsets, dtype=jnp.int32)
    )
    return running_top + jnp.log(running_sum)


def backward_pass(
    queries,
    out_grad,
    key_ext,
    value_ext,
    log_total,
    out_dot,
    inside_ext,
    active_ext,
    pattern,
    tile_span,
    score_scale,
):
    query_acc = jnp.zeros(queries.shape, jnp.float32)
    pair_acc = jnp.zeros((2,) + key_ext.shape, jnp.float32)

    def backward_advance(carried, offset):
        query_sum, pair_sum = carried
        offset = as_index(offset)
        allowed = allowed_mask(inside_ext, active_ext, pattern, offset, tile_span)[..., None, None]
        key_block = block_at(key_ext, offset, tile_span)
        value_block = block_at(value_ext, offset, tile_span)
        scores = tile_scores(queries, key_block, score_scale)
        probs_full = jnp.where(allowed, jnp.exp(scores - log_total[..., None]), 0.0)
        prob_grad = product("abceid,abcejd->abceij", out_grad, value_block)
        score_grad = probs_full * (prob_grad - out_dot[..., None])
        score_low = score_grad.astype(jnp.bfloat16)
        query_sum = query_sum + product("abceij,abcejd->abceid", score_low, key_block) * score_scale
        probs_low = probs_full.astype(jnp.bfloat16)
        key_part = product("abceij,abceid->abcejd", score_low, queries) * score_scale
        value_part = product("abceij,abceid->abcejd", probs_low, out_grad)
        update = jnp.stack([key_part, value_part])
        zero = as_index(0)
        starts = (zero, offset // 9, offset // 3 % 3, offset % 3, zero, zero, zero)
        current = lax.dynamic_slice(pair_sum, starts, update.shape)
        pair_sum = lax.dynamic_update_slice(pair_sum, current + update, starts)
        return ((query_sum, pair_sum), None)

    (query_acc, pair_acc), _ = lax.scan(
        backward_advance, (query_acc, pair_acc), jnp.arange(27, dtype=jnp.int32)
    )
    return (query_acc, pair_acc)


def edge_planes(pair_acc, axis_pos):
    inner_count = pair_acc.shape[axis_pos] - 2
    upper_rim = lax.index_in_dim(pair_acc, inner_count + 1, axis=axis_pos, keepdims=False)
    lower_rim = lax.index_in_dim(pair_acc, 0, axis=axis_pos, keepdims=False)
    return (upper_rim, lower_rim)


def settle(pair_acc, axis_pos, from_below, from_above):
    inner_count = pair_acc.shape[axis_pos] - 2
    interior = lax.slice_in_dim(pair_acc, 1, inner_count + 1, axis=axis_pos)
    lead_widths = [(0, 0)] * interior.ndim
    lead_widths[axis_pos] = (0, inner_count - 1)
    tail_widths = [(0, 0)] * interior.ndim
    tail_widths[axis_pos] = (inner_count - 1, 0)
    lead_plane = jnp.pad(jnp.expand_dims(from_below, axis_pos), lead_widths)
    tail_plane = jnp.pad(jnp.expand_dims(from_above, axis_pos), tail_widths)
    return interior + lead_plane + tail_plane


def fold_time(pair_acc):
    upper_rim, lower_rim = edge_planes(pair_acc, 1)
    from_below = from_behind(upper_rim, "ta", 1)
    from_above = from_behind(lower_rim, "ta", -1)
    return settle(pair_acc, 1, from_below, from_above)


def fold_height(pair_acc):
    upper_rim, lower_rim = edge_planes(pair_acc, 2)
    from_below = from_behind(upper_rim, "ha", 1)
    from_above = from_behind(lower_rim, "ha", -1)
    return settle(pair_acc, 2, from_below, from_above)


def fold_width(pair_acc):
    upper_rim, lower_rim = edge_planes(pair_acc, 3)
    from_below = from_behind(upper_rim, "wa", 1)
    from_above = from_behind(lower_rim, "wa", -1)
    return settle(pair_acc, 3, from_below, from_above)


def on_device(queries, key_tiles, value_tiles, forward_out, out_grad, pattern, tile_active):
    width_tiles = queries.shape[2]
    score_scale = 1.0 / math.sqrt(queries.shape[5])
    tile_span = (1, 1, width_tiles)
    corner = (
        as_index(lax.axis_index("ta")),
        as_index(lax.axis_index("ha")),
        as_index(lax.axis_index("wa")) * width_tiles,
    )
    window_shape = (3, 3, width_tiles + 2)
    active_ext = lax.dynamic_slice(jnp.pad(tile_active, 1), corner, window_shape)
    inside_ext = lax.dynamic_slice(jnp.pad(jnp.ones_like(tile_active), 1), corner, window_shape)
    out_dot = jnp.sum(out_grad.astype(jnp.float32) * forward_out.astype(jnp.float32), axis=-1)
    both_ext = with_halo(jnp.stack([key_tiles, value_tiles]), (("ta", 1), ("ha", 2), ("wa", 3)), 1)
    key_ext = both_ext[0]
    value_ext = both_ext[1]
    log_total = softmax_stats(
        queries, key_ext, inside_ext, active_ext, pattern, tile_span, score_scale
    )
    query_acc, pair_acc = backward_pass(
        queries,
        out_grad,
        key_ext,
        value_ext,
        log_total,
        out_dot,
        inside_ext,
        active_ext,
        pattern,
        tile_span,
        score_scale,
    )
    interior = fold_width(fold_height(fold_time(pair_acc)))
    return (
        query_acc.astype(jnp.bfloat16),
        interior[0].astype(jnp.bfloat16),
        interior[1].astype(jnp.bfloat16),
    )


def solution(mesh):
    placed = (
        P("ta", "ha", "wa", None, None, None),
        P("ta", "ha", "wa", None, None, None),
        P("ta", "ha", "wa", None, None, None),
        P("ta", "ha", "wa", None, None, None),
        P("ta", "ha", "wa", None, None, None),
        P(),
        P(),
    )
    return jax.shard_map(
        on_device,
        mesh=mesh,
        in_specs=placed,
        out_specs=(
            P("ta", "ha", "wa", None, None, None),
            P("ta", "ha", "wa", None, None, None),
            P("ta", "ha", "wa", None, None, None),
        ),
        check_vma=False,
    )
```

profile of v0, /device:TPU:121, one launch (start us, length us, event | category | flops | bytes accessed | tf_op | source)
XLA Modules:
  0.0 847.3 jit_solution(9435749347353042395)
XLA Ops:
  1.7 2.6 collective-permute-start.1
  4.3 3.0 collective-permute-start
  7.3 3.5 collective-permute-done.1
  15.2 4.8 collective-permute-start.2
  20.0 20.6 %collective-permute-done.3 = bf16[2,3,1,2,1,384,128]{6,5,3,2,1,4,0:T(8,128)(2,1)S(1)} collective-permute-done((bf16[2,3,1,2,1,384,128]{6,5,3,2,1,4,0:T(8,128)(2,1)S(1)}, bf16[2,3,1,2,1,384,128]{6,5,3,2,1,4,0:T(8,128)(2,1)S(1)}, u32[]{:S(2)}, u32[]{:S(2)}) %collective-permute-start.3) | collective-permute-done | bytes 1179680 | tf_op jit(solution)/shard_map/ppermute | solution.py:28
  43.8 2.2 fusion.38
  46.0 4.3 collective-permute-start.4
  54.6 31.8 %collective-permute-done.4 = bf16[2,3,3,1,1,384,128]{6,5,3,2,1,4,0:T(8,128)(2,1)} collective-permute-done((bf16[2,3,3,1,1,384,128]{6,5,3,2,1,4,0:T(8,128)(2,1)}, bf16[2,3,3,1,1,384,128]{6,5,3,2,1,4,0:T(8,128)(2,1)}, u32[]{:S(2)}, u32[]{:S(2)}) %collective-permute-start.4) | collective-permute-done | bytes 1769504 | tf_op jit(solution)/shard_map/ppermute | solution.py:26
  86.4 7.7 collective-permute-done.5
  94.2 3.4 pad_maximum_fusion
  97.6 3.3 slice_bitcast_fusion.2
  100.8 239.1 %while.32 = (s32[]{:T(128)}, f32[1,1,2,1,384]{4,2,3,1,0:T(2,128)S(1)}, f32[1,1,2,1,384]{4,2,3,1,0:T(2,128)S(1)}, s32[3,3,4]{2,1,0:T(4,128)}, s32[1,27]{1,0:T(1,1...) while((s32[]{:T(128)}, ...), condition=%wide.region_5.6_spmd.clone, body=%wide.region_2.5_spmd.sunk.clone.sunk | while | flops 76973616 | bytes 2793059 | solution.py:84
  340.0 6.8 broadcast_in_dim.68
  346.8 386.1 %while.33 = (s32[]{:T(128)}, f32[1,1,2,1,384,128]{5,4,2,3,1,0:T(8,128)S(1)}, f32[2,3,3,4,1,384,128]{6,5,3,4,2,1,0:T(8,128)}, s32[27]{0:T(128)S(1)}, s32[3,3,4]{2...) while((s32[]{:T(128)}, ...), condition=%wide.region_8.9_spmd.clone, body=%wide.region_7.8_spmd.clone.sunk | while | flops 380338240 | bytes 10623665 | solution.py:128
  732.9 6.7 slice_bitcast_fusion.1
  741.5 2.7 collective-permute-start.7
  744.2 48.6 %collective-permute-done.6 = f32[2,3,4,1,384,128]{5,4,0,2,1,3:T(8,128)S(1)} collective-permute-done((f32[2,3,4,1,384,128]{5,4,0,2,1,3:T(8,128)}, f32[2,3,4,1,384,128]{5,4,0,2,1,3:T(8,128)S(1)}, u32[]{:S(2)}, u32[]{:S(2)}) %collective-permute-start.6) | collective-permute-done | bytes 4718624 | tf_op jit(solution)/shard_map/ppermute | solution.py:15
  792.9 8.3 collective-permute-done.7
  801.2 3.3 fusion.29
  804.8 5.3 collective-permute-start.8
  812.0 15.4 %collective-permute-done.8 = f32[2,1,4,1,384,128]{5,4,0,2,3,1:T(8,128)S(1)} collective-permute-done((f32[2,1,4,1,384,128]{5,4,0,2,3,1:T(8,128)S(1)}, f32[2,1,4,1,384,128]{5,4,0,2,3,1:T(8,128)S(1)}, u32[]{:S(2)}, u32[]{:S(2)}) %collective-permute-start.8) | collective-permute-done | bytes 1572896 | tf_op jit(solution)/shard_map/ppermute | solution.py:15
  827.4 5.0 collective-permute-done.9
  834.7 7.0 collective-permute-start.10
  842.4 2.5 collective-permute-done.11
  (494 shorter events, 374.7 us)
Async XLA Ops:
  1.7 9.1 %collective-permute-start.1 = (bf16[2,1,1,2,1,384,128]{6,5,3,2,1,4,0:T(8,128)(2,1)S(1)}, bf16[2,1,1,2,1,384,128]{6,5,3,2,1,4,0:T(8,128)(2,1)S(1)}, u32[]{:S(2)}, u32[]{:S(2)}) collective-permute-start(bf16[2,1,1,2,1,384,128]{6,5,3,2,1,4,0:T(8,128)(2,1)S(1)} %pad_maximum_fusion.3), channel_id=1, source_target_pairs={{64,0},{128,64},{192,128},{65,1},{129,65},{193,129},{66,2},{130,66... | collective-permute-start | bytes 1179656 | tf_op jit(solution)/shard_map/ppermute | solution.py:28
  4.3 7.7 collective-permute-start
  10.8 32.9 %copy-start.3 = (bf16[2,1,1,2,1,384,128]{6,5,3,2,1,4,0:T(8,128)(2,1)}, bf16[2,1,1,2,1,384,128]{6,5,3,2,1,4,0:T(8,128)(2,1)S(1)}, u32[]{:S(2)}) copy-start(bf16[2,1,1,2,1,384,128]{6,5,3,2,1,4,0:T(8,128)(2,1)S(1)} %collective-permute-done.1) | copy-start | bytes 1179652
  12.0 30.3 %copy-start.4 = (bf16[2,1,1,2,1,384,128]{6,5,3,2,1,4,0:T(8,128)(2,1)}, bf16[2,1,1,2,1,384,128]{6,5,3,2,1,4,0:T(8,128)(2,1)S(1)}, u32[]{:S(2)}) copy-start(bf16[2,1,1,2,1,384,128]{6,5,3,2,1,4,0:T(8,128)(2,1)S(1)} %collective-permute-done) | copy-start | bytes 1179652
  13.3 27.3 %collective-permute-start.3 = (bf16[2,3,1,2,1,384,128]{6,5,3,2,1,4,0:T(8,128)(2,1)S(1)}, bf16[2,3,1,2,1,384,128]{6,5,3,2,1,4,0:T(8,128)(2,1)S(1)}, u32[]{:S(2)}, u32[]{:S(2)}) collective-permute-start(bf16[2,3,1,2,1,384,128]{6,5,3,2,1,4,0:T(8,128)(2,1)S(1)} %pad_maximum_fusion.2), channel_id=1, source_target_pairs={{8,0},{16,8},{24,16},{32,24},{40,32},{48,40},{56,48},{9,1},{17,9},... | collective-permute-start | bytes 3538952 | tf_op jit(solution)/shard_map/ppermute | solution.py:28
  15.2 27.1 %collective-permute-start.2 = (bf16[2,3,1,2,1,384,128]{6,5,3,2,1,4,0:T(8,128)(2,1)S(1)}, bf16[2,3,1,2,1,384,128]{6,5,3,2,1,4,0:T(8,128)(2,1)S(1)}, u32[]{:S(2)}, u32[]{:S(2)}) collective-permute-start(bf16[2,3,1,2,1,384,128]{6,5,3,2,1,4,0:T(8,128)(2,1)S(1)} %pad_maximum_fusion.2), channel_id=1, source_target_pairs={{0,8},{8,16},{16,24},{24,32},{32,40},{40,48},{48,56},{1,9},{9,17},... | collective-permute-start | bytes 3538952 | tf_op jit(solution)/shard_map/ppermute | solution.py:26
  43.8 8.5 %copy-start.6 = (s32[4,8,16]{2,1,0:T(8,128)S(1)}, s32[4,8,16]{2,1,0:T(8,128)}, u32[]{:S(2)}) copy-start(s32[4,8,16]{2,1,0:T(8,128)} %param.18) | copy-start | bytes 6148
  43.8 9.2 %copy-start = (bf16[1,1,2,1,384,128]{5,4,3,2,1,0:T(8,128)(2,1)S(1)}, bf16[1,1,2,1,384,128]{5,4,3,2,1,0:T(8,128)(2,1)}, u32[]{:S(2)}) copy-start(bf16[1,1,2,1,384,128]{5,4,3,2,1,0:T(8,128)(2,1)} %param.16) | copy-start | bytes 589828
  43.8 10.3 %copy-start.1 = (bf16[1,1,2,1,384,128]{5,4,3,2,1,0:T(8,128)(2,1)S(1)}, bf16[1,1,2,1,384,128]{5,4,3,2,1,0:T(8,128)(2,1)}, u32[]{:S(2)}) copy-start(bf16[1,1,2,1,384,128]{5,4,3,2,1,0:T(8,128)(2,1)} %param.12) | copy-start | bytes 589828
  43.8 10.3 %copy-start.2 = (bf16[1,1,2,1,384,128]{5,4,3,2,1,0:T(8,128)(2,1)S(1)}, bf16[1,1,2,1,384,128]{5,4,3,2,1,0:T(8,128)(2,1)}, u32[]{:S(2)}) copy-start(bf16[1,1,2,1,384,128]{5,4,3,2,1,0:T(8,128)(2,1)} %param.13) | copy-start | bytes 589828
  43.8 50.4 %copy-start.5 = (bf16[1,1,2,1,384,128]{5,4,3,2,1,0:T(8,128)(2,1)S(1)}, bf16[1,1,2,1,384,128]{5,4,3,2,1,0:T(8,128)(2,1)}, u32[]{:S(2)}) copy-start(bf16[1,1,2,1,384,128]{5,4,3,2,1,0:T(8,128)(2,1)} %param.14) | copy-start | bytes 589828
  46.0 40.4 %collective-permute-start.4 = (bf16[2,3,3,1,1,384,128]{6,5,3,2,1,4,0:T(8,128)(2,1)}, bf16[2,3,3,1,1,384,128]{6,5,3,2,1,4,0:T(8,128)(2,1)}, u32[]{:S(2)}, u32[]{:S(2)}) collective-permute-start(bf16[2,3,3,1,1,384,128]{6,5,3,2,1,4,0:T(8,128)(2,1)} %get-tuple-element.503), channel_id=1, source_target_pairs={{0,1},{1,2},{2,3},{3,4},{4,5},{5,6},{6,7},{8,9},{9,10},{10,11},{11... | collective-permute-start | bytes 5308424 | tf_op jit(solution)/shard_map/ppermute | solution.py:26
  50.3 43.8 %collective-permute-start.5 = (bf16[2,3,3,1,1,384,128]{6,5,3,2,1,4,0:T(8,128)(2,1)}, bf16[2,3,3,1,1,384,128]{6,5,3,2,1,4,0:T(8,128)(2,1)}, u32[]{:S(2)}, u32[]{:S(2)}) collective-permute-start(bf16[2,3,3,1,1,384,128]{6,5,3,2,1,4,0:T(8,128)(2,1)} %get-tuple-element.504), channel_id=1, source_target_pairs={{1,0},{2,1},{3,2},{4,3},{5,4},{6,5},{7,6},{9,8},{10,9},{11,10},{12... | collective-permute-start | bytes 5308424 | tf_op jit(solution)/shard_map/ppermute | solution.py:28
  97.5 3.3 copy-start.7
  97.5 3.3 copy-start.8
  739.6 53.3 %collective-permute-start.6 = (f32[2,3,4,1,384,128]{5,4,0,2,1,3:T(8,128)}, f32[2,3,4,1,384,128]{5,4,0,2,1,3:T(8,128)S(1)}, u32[]{:S(2)}, u32[]{:S(2)}) collective-permute-start(f32[2,3,4,1,384,128]{5,4,0,2,1,3:T(8,128)} %get-tuple-element.497), channel_id=1, source_target_pairs={{0,64},{64,128},{128,192},{1,65},{65,129},{129,193},{2,66},{66,130... | collective-permute-start | bytes 14155784 | tf_op jit(solution)/shard_map/ppermute | solution.py:15
  741.5 59.7 %collective-permute-start.7 = (f32[2,3,4,1,384,128]{5,4,0,2,1,3:T(8,128)S(1)}, f32[2,3,4,1,384,128]{5,4,0,2,1,3:T(8,128)S(1)}, u32[]{:S(2)}, u32[]{:S(2)}) collective-permute-start(f32[2,3,4,1,384,128]{5,4,0,2,1,3:T(8,128)S(1)} %get-tuple-element.498), channel_id=1, source_target_pairs={{64,0},{128,64},{192,128},{65,1},{129,65},{193,129},{66,2},{130,66... | collective-permute-start | bytes 14155784 | tf_op jit(solution)/shard_map/ppermute | solution.py:15
  804.8 22.7 %collective-permute-start.8 = (f32[2,1,4,1,384,128]{5,4,0,2,3,1:T(8,128)S(1)}, f32[2,1,4,1,384,128]{5,4,0,2,3,1:T(8,128)S(1)}, u32[]{:S(2)}, u32[]{:S(2)}) collective-permute-start(f32[2,1,4,1,384,128]{5,4,0,2,3,1:T(8,128)S(1)} %get-tuple-element.501), channel_id=1, source_target_pairs={{0,8},{8,16},{16,24},{24,32},{32,40},{40,48},{48,56},{1,9},{9,17},... | collective-permute-start | bytes 4718600 | tf_op jit(solution)/shard_map/ppermute | solution.py:15
  810.1 22.4 %collective-permute-start.9 = (f32[2,1,4,1,384,128]{5,4,0,2,3,1:T(8,128)S(1)}, f32[2,1,4,1,384,128]{5,4,0,2,3,1:T(8,128)S(1)}, u32[]{:S(2)}, u32[]{:S(2)}) collective-permute-start(f32[2,1,4,1,384,128]{5,4,0,2,3,1:T(8,128)S(1)} %get-tuple-element.502), channel_id=1, source_target_pairs={{8,0},{16,8},{24,16},{32,24},{40,32},{48,40},{56,48},{9,1},{17,9},... | collective-permute-start | bytes 4718600 | tf_op jit(solution)/shard_map/ppermute | solution.py:15
  832.7 12.1 %collective-permute-start.11 = (f32[2,1,1,1,384,128]{5,4,0,3,2,1:T(8,128)S(1)}, f32[2,1,1,1,384,128]{5,4,0,3,2,1:T(8,128)S(1)}, u32[]{:S(2)}, u32[]{:S(2)}) collective-permute-start(f32[2,1,1,1,384,128]{5,4,0,3,2,1:T(8,128)S(1)} %get-tuple-element.505), channel_id=1, source_target_pairs={{1,0},{2,1},{3,2},{4,3},{5,4},{6,5},{7,6},{9,8},{10,9},{11,10},{12... | collective-permute-start | bytes 1179656 | tf_op jit(solution)/shard_map/ppermute | solution.py:15
  834.7 11.7 %collective-permute-start.10 = (f32[2,1,1,1,384,128]{5,4,0,3,2,1:T(8,128)S(1)}, f32[2,1,1,1,384,128]{5,4,0,3,2,1:T(8,128)S(1)}, u32[]{:S(2)}, u32[]{:S(2)}) collective-permute-start(f32[2,1,1,1,384,128]{5,4,0,3,2,1:T(8,128)S(1)} %get-tuple-element.506), channel_id=1, source_target_pairs={{0,1},{1,2},{2,3},{3,4},{4,5},{5,6},{6,7},{8,9},{9,10},{10,11},{11... | collective-permute-start | bytes 1179656 | tf_op jit(solution)/shard_map/ppermute | solution.py:15
where the time goes:
time: 862 us; the launch traced here: 847 us
  loops' own time  273 us (32%)
  other arithmetic  179 us (21%)
  matrix products  155 us (18%)
  waiting for transfers between devices  148 us (17%)
  local copies, waits for them, and re-layouts  51.5 us (6%)
  starting transfers between devices  39.2 us (5%)
    dot_general x162, matrix products, product(): return jnp.einsum(form, left, right, preferred_element_type=jnp.float32)  155 us
    another operation x1, loops' own time, backward_pass(): lax.scan(backward_advance, (query_acc, pair_acc), jnp.arange(27, dtype=jn...  139 us
    another operation x1, loops' own time, softmax_stats(): lax.scan(softmax_advance, (running_top, running_sum), jnp.asarray(side_of...  134 us
    ppermute x6, waiting for transfers between devices, from_behind(): return lax.ppermute(x, axis, pairs)  81.4 us
    and x53, other arithmetic, allowed_mask(): return (inside_here[..., None] == 1) & ((offset == 13) | listed)  72.7 us
    dynamic_update_slice x27, other arithmetic, backward_advance(): pair_sum = lax.dynamic_update_slice(pair_sum, current + update, starts)  57.5 us
    ppermute x3, waiting for transfers between devices, with_halo(): lax.ppermute(tail, axis, [(i, (i + 1) % count) for i in range(ends)])  34.7 us
    ppermute x3, waiting for transfers between devices, with_halo(): lax.ppermute(head, axis, [((i + 1) % count, i) for i in range(ends)])  31.8 us
  transfers between devices with their start and end apart: 12, of which 12 were waited for; matrix products, arithmetic and copies ran while one was open for 0% of the time, Pallas kernels for 0%

commit v1 on v0

v1 whole, which is shorter than its diff:
```python
import functools
import math

import jax
import jax.numpy as jnp
from jax import lax
from jax.experimental import pallas as pl
from jax.experimental.pallas import tpu as pltpu
from jax.sharding import PartitionSpec as P

MESH = pl.DeviceIdType.MESH
F32 = jnp.float32
BF16 = jnp.bfloat16
NT = (((1,), (1,)), ((), ()))
TN = (((0,), (0,)), ((), ()))
NN = (((1,), (0,)), ((), ()))
LOW = -1e30
TOGETHER = 3


def dot(left, right, form):
    return lax.dot_general(left, right, form, preferred_element_type=F32)


def position():
    return lax.axis_index("ta"), lax.axis_index("ha"), lax.axis_index("wa")


class Links:
    def __init__(self, sizes, send_sem, recv_sem):
        self.sizes = sizes
        self.at = position()
        self.send_sem = send_sem
        self.recv_sem = recv_sem

    def there(self, step):
        found = None
        for place, size, by in zip(self.at, self.sizes, step):
            if by:
                ok = (place + by >= 0) & (place + by < size)
                found = ok if found is None else found & ok
        return found

    def device(self, step):
        return tuple(
            lax.rem(place + by + size, size) for place, size, by in zip(self.at, self.sizes, step)
        )

    def greet(self, steps):
        barrier = pltpu.get_barrier_semaphore()
        count = 0
        for step in steps:
            count = count + self.there(step).astype(jnp.int32)

            @pl.when(self.there(step))
            def _():
                pl.semaphore_signal(
                    barrier, inc=1, device_id=self.device(step), device_id_type=MESH
                )

        pl.semaphore_wait(barrier, count)

    def copy(self, src, dst, number, step):
        return pltpu.make_async_remote_copy(
            src_ref=src,
            dst_ref=dst,
            send_sem=self.send_sem.at[number],
            recv_sem=self.recv_sem.at[number],
            device_id=self.device(step),
            device_id_type=MESH,
        )


def back(step):
    return tuple(-by for by in step)


W_UP, W_DOWN, T_UP, T_DOWN, H_UP, H_DOWN = (
    (0, 0, 1),
    (0, 0, -1),
    (1, 0, 0),
    (-1, 0, 0),
    (0, 1, 0),
    (0, -1, 0),
)


def gather_kernel(sizes, q, do, k, v, qa, doa, ka, va, local_sem, send_sem, recv_sem):
    links = Links(sizes, send_sem, recv_sem)
    there = links.there
    links.greet([W_UP, W_DOWN, T_UP, T_DOWN, H_UP, H_DOWN])
    locals_ = []
    plain = []
    relays = []
    number = 0
    for turn, (rows, rows_all, cols, cols_all) in enumerate(((q, qa, k, ka), (do, doa, v, va))):
        to_right = links.copy(rows.at[1], rows_all.at[1, 0], number, W_UP)
        to_left = links.copy(rows.at[0], rows_all.at[1, 3], number + 1, W_DOWN)
        plain += [
            (to_right, there(W_UP), None),
            (to_left, there(W_DOWN), None),
            (links.copy(rows, rows_all.at[0, pl.ds(1, 2)], number + 2, T_UP), there(T_UP), there(T_DOWN)),
            (links.copy(rows, rows_all.at[2, pl.ds(1, 2)], number + 3, T_DOWN), there(T_DOWN), there(T_UP)),
            (links.copy(cols, cols_all.at[0], number + 4, H_UP), there(H_UP), there(H_DOWN)),
            (links.copy(cols, cols_all.at[2], number + 5, H_DOWN), there(H_DOWN), there(H_UP)),
        ]
        number += 6
        for came, spot, has in ((to_right, 0, there(W_DOWN)), (to_left, 3, there(W_UP))):
            fans = []
            for step, slot in ((T_UP, 0), (T_DOWN, 2)):
                fan = links.copy(rows_all.at[1, spot], rows_all.at[slot, spot], number, step)
                fans.append((fan, has & there(step), has & there(back(step))))
                number += 1
            relays.append((came, has, fans))
        locals_ += [
            pltpu.make_async_copy(rows, rows_all.at[1, pl.ds(1, 2)], local_sem.at[2 * turn]),
            pltpu.make_async_copy(cols, cols_all.at[1], local_sem.at[2 * turn + 1]),
        ]
    for copy, goes, _ in plain:
        pl.when(goes)(copy.start)
    for copy in locals_:
        copy.start()
    for came, has, fans in relays:
        pl.when(has)(came.wait_recv)
        for fan, goes, _ in fans:
            pl.when(goes)(fan.start)
    for copy, goes, comes in plain + [fan for _, _, fans in relays for fan in fans]:
        pl.when(goes)(copy.wait_send)
        if comes is not None:
            pl.when(comes)(copy.wait_recv)
    for copy in locals_:
        copy.wait()


def list_pairs(sizes, pattern, active, pairs):
    t, h, w = position()
    nt, nh, nw = sizes

    def keys(place, count):
        row, col = place // 2, place % 2
        key_in = (h + row - 1 >= 0) & (h + row - 1 < nh)
        key_h = jnp.clip(h + row - 1, 0, nh - 1)
        lit = active[t * nh + key_h, 2 * w + col]
        for time in range(3):
            time_in = (t + time - 1 >= 0) & (t + time - 1 < nt)
            for shift in range(3):
                spot = col + 2 - shift
                inside = key_in & time_in & (2 * w + spot - 1 >= 0) & (2 * w + spot - 1 < 2 * nw)
                offset = 9 * (2 - time) + 3 * row + shift
                chosen = (pattern[0, offset] == 1) & (lit == 1)
                pairs[count] = place * 12 + time * 4 + spot
                count = count + (inside & (chosen | (offset == 13))).astype(jnp.int32)
        return count

    return lax.fori_loop(0, 6, keys, jnp.int32(0))


def pair_at(pairs, count, index):
    real = index < count
    code = jnp.where(real, pairs[jnp.minimum(index, count - 1)], 0)
    key, query = code // 12, code % 12
    return key, query, jnp.where(real, key, 6), jnp.where(real, query, 12)


def stats_kernel(sizes, factor, pattern, active, q, k, do, fo, out, pairs, acc):
    count = list_pairs(sizes, pattern, active, pairs)
    acc[:, 0:1, :] = jnp.full((13, 1, acc.shape[2]), LOW, F32)
    acc[:, 1:8, :] = jnp.zeros((13, 7, acc.shape[2]), F32)
    for tile in range(2):
        both = do[tile].astype(F32) * fo[tile].astype(F32)
        acc[5 + tile, 2:3, :] = jnp.sum(both.T, axis=0, keepdims=True)

    def some(group, carried):
        spots = [pair_at(pairs, count, group * TOGETHER + x) for x in range(TOGETHER)]
        scores = [dot(k[key], q[query], NT) * factor for key, query, _, _ in spots]
        tops = [jnp.max(x, axis=0, keepdims=True) for x in scores]
        sums = [jnp.sum(jnp.exp2(x - top), axis=0, keepdims=True) for x, top in zip(scores, tops)]
        for (_, _, _, query), top, total in zip(spots, tops, sums):
            old = acc[query, 0:1, :]
            new = jnp.maximum(old, top)
            acc[query, 1:2, :] = acc[query, 1:2, :] * jnp.exp2(old - new) + total * jnp.exp2(top - new)
            acc[query, 0:1, :] = new
        return carried

    lax.fori_loop(0, pl.cdiv(count, TOGETHER), some, 0)
    out[...] = acc[0:12]


PLANE = [(dt, dw) for dt in (-1, 0, 1) for dw in (-1, 0, 1) if (dt, dw) != (0, 0)]


def totals_kernel(sizes, part, out, inbox, send_sem, recv_sem):
    links = Links(sizes, send_sem, recv_sem)
    links.greet([(dt, 0, dw) for dt, dw in PLANE])
    first = []
    second = []
    for number, (dt, dw) in enumerate(PLANE):
        step = (dt, 0, dw)
        goes, comes = links.there(step), links.there(back(step))
        if dw == 0:
            src, dst = part.at[1 + dt, pl.ds(1, 2)], inbox.at[number]
            own, far = out.at[1, pl.ds(1, 2)], out.at[1 - dt, pl.ds(1, 2)]
        elif dw == 1:
            src, dst = part.at[1 + dt, 3], inbox.at[number, 0]
            own, far = out.at[1, 2], out.at[1 - dt, 0]
        else:
            src, dst = part.at[1 + dt, 0], inbox.at[number, 1]
            own, far = out.at[1, 1], out.at[1 - dt, 3]
        copy = links.copy(src, dst, number, step)
        pl.when(goes)(copy.start)
        first.append((copy, goes, comes, dst))
        second.append((links.copy(own, far, 8 + number, step), goes, comes))
    for copy, goes, comes, dst in first:

        @pl.when(jnp.logical_not(comes))
        def _():
            dst[...] = jnp.full(dst.shape, LOW, F32)

        pl.when(comes)(copy.wait_recv)
    for tile in range(2):
        terms = [(part[1, 1 + tile, 0:1, :], part[1, 1 + tile, 1:2, :])]
        for number, (dt, dw) in enumerate(PLANE):
            if dw == 0 or dw == 1 - 2 * tile:
                total = inbox[number, tile, 1:2, :]
                terms.append((inbox[number, tile, 0:1, :], jnp.maximum(total, 0.0)))
        top = functools.reduce(jnp.maximum, [x for x, _ in terms])
        total = sum(x * jnp.exp2(y - top) for y, x in terms)
        out[1, 1 + tile, 0:1, :] = top + jnp.log2(total)
        out[1, 1 + tile, 1:2, :] = part[1, 1 + tile, 2:3, :]
        out[1, 1 + tile, 2:8, :] = jnp.zeros((6, out.shape[3]), F32)
    for copy, goes, _ in second:
        pl.when(goes)(copy.start)
    for copy, goes, _, _ in first:
        pl.when(goes)(copy.wait_send)
    for copy, goes, comes in second:
        pl.when(goes)(copy.wait_send)
        pl.when(comes)(copy.wait_recv)


def grads_kernel(sizes, factor, pattern, active, q, do, k, v, ld, dqa, dka, dva, pairs, dq, dk, dv):
    count = list_pairs(sizes, pattern, active, pairs)

    def clear(tile, carried):
        dq[tile] = jnp.zeros(dq.shape[1:], F32)

        @pl.when(tile < 6)
        def _():
            dk[tile] = jnp.zeros(dk.shape[1:], F32)
            dv[tile] = jnp.zeros(dv.shape[1:], F32)

        return carried

    lax.fori_loop(0, 12, clear, 0)

    def some(group, carried):
        spots = [pair_at(pairs, count, group * TOGETHER + x) for x in range(TOGETHER)]
        scores = [dot(k[key], q[query], NT) for key, query, _, _ in spots]
        slopes = [dot(v[key], do[query], NT) for key, query, _, _ in spots]
        probs = [jnp.exp2(x * factor - ld[query, 0:1, :]) for x, (_, query, _, _) in zip(scores, spots)]
        grads = [p * (x - ld[query, 1:2, :]) for p, x, (_, query, _, _) in zip(probs, slopes, spots)]
        probs = [x.astype(BF16) for x in probs]
        grads = [x.astype(BF16) for x in grads]
        values = [dot(x, do[query], NN) for x, (_, query, _, _) in zip(probs, spots)]
        keys = [dot(x, q[query], NN) for x, (_, query, _, _) in zip(grads, spots)]
        queries = [dot(k[key], x, TN) for x, (key, _, _, _) in zip(grads, spots)]
        for (_, _, key, query), x, y, z in zip(spots, queries, keys, values):
            dq[query] += x
            dk[key] += y
            dv[key] += z
        return carried

    lax.fori_loop(0, pl.cdiv(count, TOGETHER), some, 0)

    def finish(tile, carried):
        dqa[tile] = dq[tile].astype(BF16)

        @pl.when(tile < 6)
        def _():
            dka[tile] = dk[tile].astype(BF16)
            dva[tile] = dv[tile].astype(BF16)

        return carried

    lax.fori_loop(0, 12, finish, 0)


def return_kernel(
    sizes, scale, dqa, dka, dva, dq, dk, dv, time_in, key_in, value_in, edge, width_in, send_sem, recv_sem
):
    links = Links(sizes, send_sem, recv_sem)
    there = links.there
    links.greet([W_UP, W_DOWN, T_UP, T_DOWN, H_UP, H_DOWN])
    copies = []
    for number, (src, dst, step) in enumerate(
        (
            (dqa.at[2], time_in.at[0], T_UP),
            (dqa.at[0], time_in.at[1], T_DOWN),
            (dka.at[2], key_in.at[0], H_UP),
            (dka.at[0], key_in.at[1], H_DOWN),
            (dva.at[2], value_in.at[0], H_UP),
            (dva.at[0], value_in.at[1], H_DOWN),
        )
    ):
        copy = links.copy(src, dst, number, step)
        pl.when(there(step))(copy.start)
        copies.append((copy, step, dst))
    edges = []
    for number, (src, dst, step) in enumerate(
        ((edge.at[1], width_in.at[0], W_UP), (edge.at[0], width_in.at[1], W_DOWN))
    ):
        edges.append((links.copy(src, dst, 6 + number, step), step, dst))

    def take(entry):
        copy, step, dst = entry
        comes = there(back(step))

        @pl.when(jnp.logical_not(comes))
        def _():
            dst[...] = jnp.zeros(dst.shape, dst.dtype)

        pl.when(comes)(copy.wait_recv)

    take(copies[0])
    take(copies[1])
    for spot, column in ((0, 0), (1, 3)):
        total = dqa[1, column].astype(F32) + time_in[0, column].astype(F32) + time_in[1, column].astype(F32)
        edge[spot] = total.astype(BF16)
    for copy, step, _ in edges:
        pl.when(there(step))(copy.start)
    for entry in copies[2:]:
        take(entry)
    for tile in range(2):
        total = dka[1, tile].astype(F32) + key_in[0, tile].astype(F32) + key_in[1, tile].astype(F32)
        dk[tile] = (total * scale).astype(BF16)
        total = dva[1, tile].astype(F32) + value_in[0, tile].astype(F32) + value_in[1, tile].astype(F32)
        dv[tile] = total.astype(BF16)
    for entry in edges:
        take(entry)
    for tile in range(2):
        total = dqa[1, 1 + tile].astype(F32) + width_in[tile].astype(F32)
        total = total + time_in[0, 1 + tile].astype(F32) + time_in[1, 1 + tile].astype(F32)
        dq[tile] = (total * scale).T.astype(BF16)
    for copy, step, _ in copies + edges:
        pl.when(there(step))(copy.wait_send)


def params(number=None, megabytes=40):
    if number is None:
        return pltpu.CompilerParams(vmem_limit_bytes=megabytes << 20)
    return pltpu.CompilerParams(
        collective_id=number, has_side_effects=True, vmem_limit_bytes=megabytes << 20
    )


def shape(*dims, dtype=BF16):
    return jax.ShapeDtypeStruct(dims, dtype)


def on_device(sizes, queries, key_tiles, value_tiles, forward_out, out_grad, pattern, tile_active):
    whole = queries.shape
    tile, feat = whole[4], whole[5]
    scale = 1.0 / math.sqrt(feat)
    factor = scale * math.log2(math.e)
    q, k, v, fo, do = (
        x.reshape(2, tile, feat) for x in (queries, key_tiles, value_tiles, forward_out, out_grad)
    )
    active = tile_active.reshape(-1, tile_active.shape[2])
    hbm = pl.BlockSpec(memory_space=pl.ANY)
    vmem = pl.BlockSpec(memory_space=pltpu.VMEM)
    smem = pl.BlockSpec(memory_space=pltpu.SMEM)
    dma = pltpu.SemaphoreType.DMA

    qa, doa, ka, va = pl.pallas_call(
        functools.partial(gather_kernel, sizes),
        out_shape=[
            shape(3, 4, tile, feat),
            shape(3, 4, tile, feat),
            shape(3, 2, tile, feat),
            shape(3, 2, tile, feat),
        ],
        in_specs=[hbm] * 4,
        out_specs=[hbm] * 4,
        scratch_shapes=[dma((4,)), dma((20,)), dma((20,))],
        compiler_params=params(0),
        name="gather",
    )(q, do, k, v)
    qa, doa = (x.reshape(12, tile, feat) for x in (qa, doa))
    ka, va = (x.reshape(6, tile, feat) for x in (ka, va))

    part = pl.pallas_call(
        functools.partial(stats_kernel, sizes, factor),
        out_shape=shape(12, 8, tile, dtype=F32),
        in_specs=[smem, smem, vmem, vmem, vmem, vmem],
        out_specs=vmem,
        scratch_shapes=[pltpu.SMEM((64,), jnp.int32), pltpu.VMEM((13, 8, tile), F32)],
        compiler_params=params(),
        name="stats",
    )(pattern, active, qa, ka, do, fo)

    ld = pl.pallas_call(
        functools.partial(totals_kernel, sizes),
        out_shape=shape(3, 4, 8, tile, dtype=F32),
        in_specs=[vmem],
        out_specs=vmem,
        scratch_shapes=[pltpu.VMEM((8, 2, 8, tile), F32), dma((16,)), dma((16,))],
        compiler_params=params(1),
        name="totals",
    )(part.reshape(3, 4, 8, tile))

    dqa, dka, dva = pl.pallas_call(
        functools.partial(grads_kernel, sizes, factor),
        out_shape=[shape(12, feat, tile), shape(6, tile, feat), shape(6, tile, feat)],
        in_specs=[smem, smem, vmem, vmem, vmem, vmem, vmem],
        out_specs=[vmem] * 3,
        scratch_shapes=[
            pltpu.SMEM((64,), jnp.int32),
            pltpu.VMEM((13, feat, tile), F32),
            pltpu.VMEM((7, tile, feat), F32),
            pltpu.VMEM((7, tile, feat), F32),
        ],
        compiler_params=params(),
        name="grads",
    )(pattern, active, qa, doa, ka, va, ld.reshape(12, 8, tile))

    dq, dk, dv = pl.pallas_call(
        functools.partial(return_kernel, sizes, scale),
        out_shape=[shape(2, tile, feat)] * 3,
        in_specs=[vmem] * 3,
        out_specs=[vmem] * 3,
        scratch_shapes=[
            pltpu.VMEM((2, 4, feat, tile), BF16),
            pltpu.VMEM((2, 2, tile, feat), BF16),
            pltpu.VMEM((2, 2, tile, feat), BF16),
            pltpu.VMEM((2, feat, tile), BF16),
            pltpu.VMEM((2, feat, tile), BF16),
            dma((8,)),
            dma((8,)),
        ],
        compiler_params=params(2),
        name="returns",
    )(dqa.reshape(3, 4, feat, tile), dka.reshape(3, 2, tile, feat), dva.reshape(3, 2, tile, feat))
    return dq.reshape(whole), dk.reshape(whole), dv.reshape(whole)


def solution(mesh):
    tiles = P("ta", "ha", "wa", None, None, None)
    sizes = tuple(mesh.shape[axis] for axis in ("ta", "ha", "wa"))
    return jax.shard_map(
        functools.partial(on_device, sizes),
        mesh=mesh,
        in_specs=(tiles,) * 5 + (P(), P()),
        out_specs=(tiles,) * 3,
        check_vma=False,
    )
```

time: 862 us -> 77.5 us (0.09); the launches traced: 847 us -> 77.3 us
  loops' own time: 273 us -> 0 us
  other arithmetic: 179 us -> 0 us
  matrix products: 155 us -> 0 us
  waiting for transfers between devices: 148 us -> 0 us
  Pallas kernels: 0 us -> 68.5 us
  local copies, waits for them, and re-layouts: 51.5 us -> 8.03 us
  starting transfers between devices: 39.2 us -> 0 us
    another operation x2 -> x0, loops' own time: 273 us -> none  [the longest x1 139 us: backward_pass(): lax.scan(backward_advance, (query_acc, pair_acc), jnp.arange(27, dtype=jn...]
    dot_general x162 -> x0, matrix products: 155 us -> none  [product(): return jnp.einsum(form, left, right, preferred_element_type=jnp.float32)]
    ppermute x12 -> x0, waiting for transfers between devices: 148 us -> none  [the longest x6 81.4 us: from_behind(): return lax.ppermute(x, axis, pairs)]
    and x53 -> x0, other arithmetic: 72.7 us -> none  [allowed_mask(): return (inside_here[..., None] == 1) & ((offset == 13) | listed)]
    pallas_call x0 -> x5, Pallas kernels: none -> 68.5 us  [the longest x1 20.8 us: on_device(): pl.pallas_call(functools.partial(return_kernel, sizes, scale), out_shape=...]
    dynamic_update_slice x27 -> x0, other arithmetic: 57.5 us -> none  [backward_advance(): pair_sum = lax.dynamic_update_slice(pair_sum, current + update, starts)]
    ppermute x12 -> x0, starting transfers between devices: 39.2 us -> none  [the longest x6 20.7 us: from_behind(): return lax.ppermute(x, axis, pairs)]
    dynamic_slice x54 -> x0, local copies, waits for them, and re-layouts: 31.3 us -> none  [the longest x27 15.5 us: backward_pass(): lax.scan(backward_advance, (query_acc, pair_acc), jnp.arange(27, dtype=jn...]
  transfers between devices with their start and end apart: 12 -> 0, of which waited for: 12 -> 0; matrix products, arithmetic and copies ran while one was open for 0% -> 0% of each run, Pallas kernels for 0% -> 0%
where the time goes in v1:
time: 77.5 us; the launch traced here: 77.3 us
  Pallas kernels  68.5 us (88%)
  local copies, waits for them, and re-layouts  8.03 us (10%)
    pallas_call x1, Pallas kernels, on_device(): pl.pallas_call(functools.partial(return_kernel, sizes, scale), out_shape=...  20.8 us
    pallas_call x1, Pallas kernels, on_device(): pl.pallas_call(functools.partial(gather_kernel, sizes), out_shape=[shape(...  18 us
    pallas_call x1, Pallas kernels, on_device(): pl.pallas_call(functools.partial(totals_kernel, sizes), out_shape=shape(3...  12.3 us
    pallas_call x1, Pallas kernels, on_device(): pl.pallas_call(functools.partial(grads_kernel, sizes, factor), out_shape=...  11.5 us
    unnamed x21, local copies, waits for them, and re-layouts  8.03 us
    pallas_call x1, Pallas kernels, on_device(): pl.pallas_call(functools.partial(stats_kernel, sizes, factor), out_shape=...  5.9 us

profile of v1, /device:TPU:121, one launch (start us, length us, event | category | flops | bytes accessed | tf_op | source)
XLA Modules:
  0.0 77.3 jit_solution(15023323322649200804)
XLA Ops:
  0.6 0.0 copy-start
  0.6 0.9 %copy-done = bf16[1,1,2,1,384,128]{5,4,3,2,1,0:T(8,128)(2,1)S(1)} copy-done((bf16[1,1,2,1,384,128]{5,4,3,2,1,0:T(8,128)(2,1)S(1)}, bf16[1,1,2,1,384,128]{5,4,3,2,1,0:T(8,128)(2,1)}, u32[]{:S(2)}) %copy-start) | copy-done | bytes 196632
  1.6 0.0 copy-start.2
  1.6 0.9 %copy-done.2 = bf16[1,1,2,1,384,128]{5,4,3,2,1,0:T(8,128)(2,1)S(1)} copy-done((bf16[1,1,2,1,384,128]{5,4,3,2,1,0:T(8,128)(2,1)S(1)}, bf16[1,1,2,1,384,128]{5,4,3,2,1,0:T(8,128)(2,1)}, u32[]{:S(2)}) %copy-start.2) | copy-done | bytes 196632
  2.5 0.0 copy-start.3
  2.5 0.9 %copy-done.3 = bf16[1,1,2,1,384,128]{5,4,3,2,1,0:T(8,128)(2,1)S(1)} copy-done((bf16[1,1,2,1,384,128]{5,4,3,2,1,0:T(8,128)(2,1)S(1)}, bf16[1,1,2,1,384,128]{5,4,3,2,1,0:T(8,128)(2,1)}, u32[]{:S(2)}) %copy-start.3) | copy-done | bytes 196632
  3.4 0.0 copy-start.4
  3.4 0.9 %copy-done.4 = bf16[1,1,2,1,384,128]{5,4,3,2,1,0:T(8,128)(2,1)S(1)} copy-done((bf16[1,1,2,1,384,128]{5,4,3,2,1,0:T(8,128)(2,1)S(1)}, bf16[1,1,2,1,384,128]{5,4,3,2,1,0:T(8,128)(2,1)}, u32[]{:S(2)}) %copy-start.4) | copy-done | bytes 196632
  4.3 18.0 %gather.1 = (bf16[3,4,384,128]{3,2,1,0:T(8,128)(2,1)S(1)}, bf16[3,4,384,128]{3,2,1,0:T(8,128)(2,1)S(1)}, bf16[3,2,384,128]{3,2,1,0:T(8,128)(2,1)S(1)}, bf16[3,2,384,128]{3,2,1,0:T(8,128)(2,1)S(1)}) custom-call(bf16[2,384,128]{2,1,0:T(8,128)(2,1)S(1)} %bitcast.41, bf16[2,384,128]{2,1,0:T(8,128)(2,1)S(1)} %bitcast.30, bf16[2,384,128]{2,1,0:T(8,128)(2,1)S(1)} %bitcast.42, ...), custom_call_target="tpu_custom_call" | custom-call | tf_op jit(solution)/shard_map/gather/pallas_call | solution.py:373
  22.4 0.0 copy-start.1
  22.4 0.9 %copy-done.1 = bf16[1,1,2,1,384,128]{5,4,3,2,1,0:T(8,128)(2,1)S(1)} copy-done((bf16[1,1,2,1,384,128]{5,4,3,2,1,0:T(8,128)(2,1)S(1)}, bf16[1,1,2,1,384,128]{5,4,3,2,1,0:T(8,128)(2,1)}, u32[]{:S(2)}) %copy-start.1) | copy-done | bytes 196632
  23.3 0.0 copy-start.5
  23.3 0.7 copy-done.5
  24.0 0.0 copy-start.7
  24.0 0.7 copy-done.7
  24.7 5.9 %stats.1 = f32[12,8,384]{2,1,0:T(8,128)S(1)} custom-call(s32[1,27]{1,0:T(1,128)S(1)} %copy-done.7, s32[32,16]{1,0:T(8,128)S(1)} %bitcast.44, bf16[12,384,128]{2,1,0:T(8,128)(2,1)S(1)} %bitcast.24, bf16[6,384,128]{2,1,0:T(8,128)(2,1)S(1)} %bitcast.26, bf16[2,384,128]{2,1,0:T(8,128)(2,1)S(1)} %bitcast.31, bf16[2,384,128]{2,1,0:T(8,128)(2,1)S(1)} %bitcast.37), custom_call_target="tpu_custom_call" | custom-call | tf_op jit(solution)/shard_map/stats/pallas_call | solution.py:390
  30.6 12.3 %totals.1 = f32[3,4,8,384]{3,2,1,0:T(8,128)S(1)} custom-call(f32[3,4,8,384]{3,2,1,0:T(8,128)S(1)} %bitcast.33), custom_call_target="tpu_custom_call" | custom-call | tf_op jit(solution)/shard_map/totals/pallas_call | solution.py:400
  42.9 0.0 copy-done.6
  42.9 0.0 copy-done.8
  42.9 11.5 %grads.1 = (bf16[12,128,384]{2,1,0:T(8,128)(2,1)S(1)}, bf16[6,384,128]{2,1,0:T(8,128)(2,1)S(1)}, bf16[6,384,128]{2,1,0:T(8,128)(2,1)S(1)}) custom-call(s32[1,27]{1,0:T(1,128)S(1)} %copy-done.8, s32[32,16]{1,0:T(8,128)S(1)} %bitcast.45, bf16[12,384,128]{2,1,0:T(8,128)(2,1)S(1)} %bitcast.25, bf16[12,384,128]{2,1,0:T(8,128)(2,1)S(1)} %bitcast.29, ...), custom_call_target="tpu_custom_call" | custom-call | tf_op jit(solution)/shard_map/grads/pallas_call | solution.py:410
  54.5 20.8 %returns.1 = (bf16[2,384,128]{2,1,0:T(8,128)(2,1)S(1)}, bf16[2,384,128]{2,1,0:T(8,128)(2,1)S(1)}, bf16[2,384,128]{2,1,0:T(8,128)(2,1)S(1)}) custom-call(bf16[3,4,128,384]{3,2,1,0:T(8,128)(2,1)S(1)} %bitcast.28, bf16[3,2,384,128]{3,2,1,0:T(8,128)(2,1)S(1)} %bitcast.34, bf16[3,2,384,128]{3,2,1,0:T(8,128)(2,1)S(1)} %bitcast.35), custom_call_target="tpu_custom_call" | custom-call | tf_op jit(solution)/shard_map/returns/pallas_call | solution.py:425
  75.2 0.7 copy.16
  75.9 0.7 copy.17
  76.6 0.7 copy.18
  (2 shorter events, 0.0 us)
Async XLA Ops:
  0.6 0.9 %copy-start = (bf16[1,1,2,1,384,128]{5,4,3,2,1,0:T(8,128)(2,1)S(1)}, bf16[1,1,2,1,384,128]{5,4,3,2,1,0:T(8,128)(2,1)}, u32[]{:S(2)}) copy-start(bf16[1,1,2,1,384,128]{5,4,3,2,1,0:T(8,128)(2,1)} %param.11) | copy-start | bytes 589828
  1.6 0.9 %copy-start.2 = (bf16[1,1,2,1,384,128]{5,4,3,2,1,0:T(8,128)(2,1)S(1)}, bf16[1,1,2,1,384,128]{5,4,3,2,1,0:T(8,128)(2,1)}, u32[]{:S(2)}) copy-start(bf16[1,1,2,1,384,128]{5,4,3,2,1,0:T(8,128)(2,1)} %param.7) | copy-start | bytes 589828
  2.5 0.9 %copy-start.3 = (bf16[1,1,2,1,384,128]{5,4,3,2,1,0:T(8,128)(2,1)S(1)}, bf16[1,1,2,1,384,128]{5,4,3,2,1,0:T(8,128)(2,1)}, u32[]{:S(2)}) copy-start(bf16[1,1,2,1,384,128]{5,4,3,2,1,0:T(8,128)(2,1)} %param.8) | copy-start | bytes 589828
  3.4 0.9 %copy-start.4 = (bf16[1,1,2,1,384,128]{5,4,3,2,1,0:T(8,128)(2,1)S(1)}, bf16[1,1,2,1,384,128]{5,4,3,2,1,0:T(8,128)(2,1)}, u32[]{:S(2)}) copy-start(bf16[1,1,2,1,384,128]{5,4,3,2,1,0:T(8,128)(2,1)} %param.9) | copy-start | bytes 589828
  22.4 0.9 %copy-start.1 = (bf16[1,1,2,1,384,128]{5,4,3,2,1,0:T(8,128)(2,1)S(1)}, bf16[1,1,2,1,384,128]{5,4,3,2,1,0:T(8,128)(2,1)}, u32[]{:S(2)}) copy-start(bf16[1,1,2,1,384,128]{5,4,3,2,1,0:T(8,128)(2,1)} %param.10) | copy-start | bytes 589828
  23.3 0.7 copy-start.5
  24.0 0.7 copy-start.7
  24.7 18.2 %copy-start.6 = (s32[4,8,16]{2,1,0:T(8,128)S(1)}, s32[4,8,16]{2,1,0:T(8,128)}, u32[]{:S(2)}) copy-start(s32[4,8,16]{2,1,0:T(8,128)} %param.13) | copy-start | bytes 6148
  24.7 18.2 %copy-start.8 = (s32[1,27]{1,0:T(1,128)S(1)}, s32[1,27]{1,0:T(1,128)}, u32[]{:S(2)}) copy-start(s32[1,27]{1,0:T(1,128)} %pattern.3) | copy-start | bytes 328

commit v2 on v1

--- a/solution.py
+++ b/solution.py
@@ -85,51 +85,163 @@
 )
 
 
-def gather_kernel(sizes, q, do, k, v, qa, doa, ka, va, local_sem, send_sem, recv_sem):
+def all_there(*conditions):
+    return functools.reduce(jnp.logical_and, conditions)
+
+
+PLANE = [(dt, dw) for dt in (-1, 0, 1) for dw in (-1, 0, 1) if (dt, dw) != (0, 0)]
+WIDE = [(dt, dw) for dt in (-2, -1, 0, 1, 2) for dw in (-1, 0, 1) if (dt, dw) != (0, 0)]
+
+
+def side_of(dw):
+    return dw % 3
+
+
+def meet_kernel(
+    sizes, factor, pattern, active, q, do, k, v, fo, qa, doa, ka, va, inbox, dots, own_fo, local_sem, send_sem, recv_sem
+):
     links = Links(sizes, send_sem, recv_sem)
     there = links.there
-    links.greet([W_UP, W_DOWN, T_UP, T_DOWN, H_UP, H_DOWN])
-    locals_ = []
-    plain = []
-    relays = []
+    t, h, w = links.at
+    nt, nh, nw = sizes
+    tile = q.shape[1]
+    row_in = [t > 0, t >= 0, t < nt - 1]
+
+    stay = [
+        pltpu.make_async_copy(src, dst, local_sem.at[spot])
+        for spot, (src, dst) in enumerate(
+            (
+                (do, doa.at[1, pl.ds(1, 2)]),
+                (fo, own_fo),
+                (q, qa.at[1, pl.ds(1, 2)]),
+                (k, ka.at[1]),
+                (v, va.at[1]),
+            )
+        )
+    ]
+    for copy in stay:
+        copy.start()
+    links.greet([(dt, 0, dw) for dt, dw in WIDE] + [H_UP, H_DOWN])
+
+    groups = []
     number = 0
-    for turn, (rows, rows_all, cols, cols_all) in enumerate(((q, qa, k, ka), (do, doa, v, va))):
-        to_right = links.copy(rows.at[1], rows_all.at[1, 0], number, W_UP)
-        to_left = links.copy(rows.at[0], rows_all.at[1, 3], number + 1, W_DOWN)
-        plain += [
-            (to_right, there(W_UP), None),
-            (to_left, there(W_DOWN), None),
+    for rows, rows_all, cols, cols_all in ((q, qa, k, ka), (do, doa, v, va)):
+        width = [
+            (links.copy(rows.at[1], rows_all.at[1, 0], number, W_UP), there(W_UP), there(W_DOWN)),
+            (links.copy(rows.at[0], rows_all.at[1, 3], number + 1, W_DOWN), there(W_DOWN), there(W_UP)),
+        ]
+        time = [
             (links.copy(rows, rows_all.at[0, pl.ds(1, 2)], number + 2, T_UP), there(T_UP), there(T_DOWN)),
             (links.copy(rows, rows_all.at[2, pl.ds(1, 2)], number + 3, T_DOWN), there(T_DOWN), there(T_UP)),
+        ]
+        height = [
             (links.copy(cols, cols_all.at[0], number + 4, H_UP), there(H_UP), there(H_DOWN)),
             (links.copy(cols, cols_all.at[2], number + 5, H_DOWN), there(H_DOWN), there(H_UP)),
         ]
         number += 6
-        for came, spot, has in ((to_right, 0, there(W_DOWN)), (to_left, 3, there(W_UP))):
-            fans = []
+        fans = []
+        for spot, has in ((0, there(W_DOWN)), (3, there(W_UP))):
             for step, slot in ((T_UP, 0), (T_DOWN, 2)):
                 fan = links.copy(rows_all.at[1, spot], rows_all.at[slot, spot], number, step)
-                fans.append((fan, has & there(step), has & there(back(step))))
+                fans.append((fan, has & there(step), has & there(back(step)), slot))
                 number += 1
-            relays.append((came, has, fans))
-        locals_ += [
-            pltpu.make_async_copy(rows, rows_all.at[1, pl.ds(1, 2)], local_sem.at[2 * turn]),
-            pltpu.make_async_copy(cols, cols_all.at[1], local_sem.at[2 * turn + 1]),
-        ]
-    for copy, goes, _ in plain:
-        pl.when(goes)(copy.start)
-    for copy in locals_:
-        copy.start()
-    for came, has, fans in relays:
-        pl.when(has)(came.wait_recv)
-        for fan, goes, _ in fans:
+        groups.append((width, time, height, fans))
+    for width, time, height, _ in groups:
+        for copy, goes, _ in width + time + height:
+            pl.when(goes)(copy.start)
+
+    stay[0].wait()
+    stay[1].wait()
+    dots[1, 0] = jnp.zeros(dots.shape[2:], F32)
+    for spot in range(2):
+        both = doa[1, 1 + spot].astype(F32) * own_fo[spot].astype(F32)
+        dots[1, 0, spot : spot + 1, :] = jnp.sum(both.T, axis=0, keepdims=True)
+    small = []
+    for dt, dw in PLANE:
+        step = (dt, 0, dw)
+        copy = links.copy(dots.at[1, 0], dots.at[1 - dt, side_of(dw)], number, step)
+        number += 1
+        pl.when(there(step))(copy.start)
+        small.append((copy, there(step), there(back(step))))
+
+    def arrive(entries):
+        for copy, _, comes in entries:
+            pl.when(comes)(copy.wait_recv)
+
+    def forward(group):
+        width, _, _, fans = group
+        arrive(width)
+        for fan, goes, _, _ in fans:
             pl.when(goes)(fan.start)
-    for copy, goes, comes in plain + [fan for _, _, fans in relays for fan in fans]:
+
+    def lit(row, col):
+        key_h = h + row - 1
+        inside = (key_h >= 0) & (key_h < nh)
+        spot = t * nh + jnp.clip(key_h, 0, nh - 1)
+        return inside, inside & (active[spot, 2 * w + col] == 1)
+
+    def totals(time, row, carried):
+        top, total = carried
+        tops = [[top[x : x + 1]] for x in range(4)]
+        scores = []
+        oks = []
+        for col in range(2):
+            inside, on = lit(row, col)
+            x = dot(ka[row, col], qa[time, pl.ds(col, 3)].reshape(3 * tile, -1), NT) * factor
+            high = jnp.max(x, axis=0, keepdims=True)
+            scores.append(x)
+            for shift in range(3):
+                offset = 9 * (2 - time) + 3 * row + 2 - shift
+                ok = (on & (pattern[0, offset] == 1)) | (inside & (offset == 13))
+                tops[col + shift].append(jnp.where(ok, high[:, shift * tile : (shift + 1) * tile], LOW))
+                oks.append(ok)
+        tops = [functools.reduce(jnp.maximum, x) for x in tops]
+        sums = [total[x : x + 1] * jnp.exp2(top[x : x + 1] - tops[x]) for x in range(4)]
+        for col in range(2):
+            part = jnp.exp2(scores[col] - jnp.concatenate(tops[col : col + 3], axis=1))
+            part = jnp.sum(part, axis=0, keepdims=True)
+            for shift in range(3):
+                term = jnp.where(oks[3 * col + shift], part[:, shift * tile : (shift + 1) * tile], 0.0)
+                sums[col + shift] = sums[col + shift] + term
+        return jnp.concatenate(tops, axis=0), jnp.concatenate(sums, axis=0)
+
+    fresh = (jnp.full((4, tile), LOW, F32), jnp.zeros((4, tile), F32))
+
+    def publish(time, carried):
+        nonlocal number
+        inbox[time, time, 0, 0:4, :], inbox[time, time, 0, 4:8, :] = carried
+        for dt in (time - 2, time - 1, time):
+            for dw in (-1, 0, 1):
+                if (dt, dw) == (0, 0):
+                    continue
+                step = (dt, 0, dw)
+                slot = inbox.at[time - dt, time, side_of(dw)]
+                copy = links.copy(inbox.at[time, time, 0], slot, number, step)
+                number += 1
+                goes = row_in[time] & there(step)
+                pl.when(goes)(copy.start)
+                small.append((copy, goes, row_in[time - dt] & there(back(step))))
+
+    stay[2].wait()
+    stay[3].wait()
+    forward(groups[0])
+    carried = totals(1, 1, fresh)
+    arrive(groups[0][2])
+    carried = lax.fori_loop(0, 2, lambda x, c: totals(1, 2 * x, c), carried)
+    publish(1, carried)
+    forward(groups[1])
+    for time, entry in ((0, 0), (2, 1)):
+        arrive([groups[0][1][entry]])
+        arrive([fan[:3] for fan in groups[0][3] if fan[3] == time])
+        publish(time, lax.fori_loop(0, 3, lambda x, c: totals(time, x, c), fresh))
+
+    arrive(groups[1][1] + groups[1][2] + [fan[:3] for fan in groups[1][3]] + small)
+    stay[4].wait()
+    for width, time, height, fans in groups:
+        for copy, goes, _ in width + time + height + [fan[:3] for fan in fans]:
+            pl.when(goes)(copy.wait_send)
+    for copy, goes, _ in small:
         pl.when(goes)(copy.wait_send)
-        if comes is not None:
-            pl.when(comes)(copy.wait_recv)
-    for copy in locals_:
-        copy.wait()
 
 
 def list_pairs(sizes, pattern, active, pairs):
@@ -162,83 +274,49 @@
     return key, query, jnp.where(real, key, 6), jnp.where(real, query, 12)
 
 
-def stats_kernel(sizes, factor, pattern, active, q, k, do, fo, out, pairs, acc):
+def join_totals(sizes, inbox, dots, ld):
+    t, h, w = position()
+    for time in range(3):
+        terms = []
+        for sender in range(3):
+            ok = (t + time - sender >= 0) & (t + time - sender < sizes[0])
+            left, right = ok & (w > 0), ok & (w < sizes[2] - 1)
+            parts = [(inbox[time, sender, 0], ok, ok)]
+            parts.append(
+                (
+                    jnp.concatenate(
+                        [
+                            inbox[time, sender, 1, 2:4, :],
+                            inbox[time, sender, 2, 0:2, :],
+                            inbox[time, sender, 1, 6:8, :],
+                            inbox[time, sender, 2, 4:6, :],
+                        ],
+                        axis=0,
+                    ),
+                    left,
+                    right,
+                )
+            )
+            for both, first, last in parts:
+                good = jnp.concatenate(
+                    [jnp.full((2, both.shape[1]), x.astype(jnp.int32)) for x in (first, last)], axis=0
+                )
+                terms.append(
+                    (jnp.where(good == 1, both[0:4], LOW), jnp.where(good == 1, both[4:8], 0.0))
+                )
+        top = functools.reduce(jnp.maximum, [x for x, _ in terms])
+        total = sum(y * jnp.exp2(x - top) for x, y in terms)
+        total = top + jnp.log2(total)
+        for spot, (side, line) in enumerate(((1, 1), (0, 0), (0, 1), (2, 0))):
+            ld[4 * time + spot, 0:1, :] = total[spot : spot + 1]
+            ld[4 * time + spot, 1:2, :] = dots[time, side, line : line + 1, :]
+
+
+def grads_kernel(
+    sizes, factor, pattern, active, q, do, k, v, inbox, dots, dqa, dka, dva, pairs, ld, dq, dk, dv
+):
     count = list_pairs(sizes, pattern, active, pairs)
-    acc[:, 0:1, :] = jnp.full((13, 1, acc.shape[2]), LOW, F32)
-    acc[:, 1:8, :] = jnp.zeros((13, 7, acc.shape[2]), F32)
-    for tile in range(2):
-        both = do[tile].astype(F32) * fo[tile].astype(F32)
-        acc[5 + tile, 2:3, :] = jnp.sum(both.T, axis=0, keepdims=True)
-
-    def some(group, carried):
-        spots = [pair_at(pairs, count, group * TOGETHER + x) for x in range(TOGETHER)]
-        scores = [dot(k[key], q[query], NT) * factor for key, query, _, _ in spots]
-        tops = [jnp.max(x, axis=0, keepdims=True) for x in scores]
-        sums = [jnp.sum(jnp.exp2(x - top), axis=0, keepdims=True) for x, top in zip(scores, tops)]
-        for (_, _, _, query), top, total in zip(spots, tops, sums):
-            old = acc[query, 0:1, :]
-            new = jnp.maximum(old, top)
-            acc[query, 1:2, :] = acc[query, 1:2, :] * jnp.exp2(old - new) + total * jnp.exp2(top - new)
-            acc[query, 0:1, :] = new
-        return carried
-
-    lax.fori_loop(0, pl.cdiv(count, TOGETHER), some, 0)
-    out[...] = acc[0:12]
-
-
-PLANE = [(dt, dw) for dt in (-1, 0, 1) for dw in (-1, 0, 1) if (dt, dw) != (0, 0)]
-
-
-def totals_kernel(sizes, part, out, inbox, send_sem, recv_sem):
-    links = Links(sizes, send_sem, recv_sem)
-    links.greet([(dt, 0, dw) for dt, dw in PLANE])
-    first = []
-    second = []
-    for number, (dt, dw) in enumerate(PLANE):
-        step = (dt, 0, dw)
-        goes, comes = links.there(step), links.there(back(step))
-        if dw == 0:
-            src, dst = part.at[1 + dt, pl.ds(1, 2)], inbox.at[number]
-            own, far = out.at[1, pl.ds(1, 2)], out.at[1 - dt, pl.ds(1, 2)]
-        elif dw == 1:
-            src, dst = part.at[1 + dt, 3], inbox.at[number, 0]
-            own, far = out.at[1, 2], out.at[1 - dt, 0]
-        else:
-            src, dst = part.at[1 + dt, 0], inbox.at[number, 1]
-            own, far = out.at[1, 1], out.at[1 - dt, 3]
-        copy = links.copy(src, dst, number, step)
-        pl.when(goes)(copy.start)
-        first.append((copy, goes, comes, dst))
-        second.append((links.copy(own, far, 8 + number, step), goes, comes))
-    for copy, goes, comes, dst in first:
-
-        @pl.when(jnp.logical_not(comes))
-        def _():
-            dst[...] = jnp.full(dst.shape, LOW, F32)
-
-        pl.when(comes)(copy.wait_recv)
-    for tile in range(2):
-        terms = [(part[1, 1 + tile, 0:1, :], part[1, 1 + tile, 1:2, :])]
-        for number, (dt, dw) in enumerate(PLANE):
-            if dw == 0 or dw == 1 - 2 * tile:
-                total = inbox[number, tile, 1:2, :]
-                terms.append((inbox[number, tile, 0:1, :], jnp.maximum(total, 0.0)))
-        top = functools.reduce(jnp.maximum, [x for x, _ in terms])
-        total = sum(x * jnp.exp2(y - top) for y, x in terms)
-        out[1, 1 + tile, 0:1, :] = top + jnp.log2(total)
-        out[1, 1 + tile, 1:2, :] = part[1, 1 + tile, 2:3, :]
-        out[1, 1 + tile, 2:8, :] = jnp.zeros((6, out.shape[3]), F32)
-    for copy, goes, _ in second:
-        pl.when(goes)(copy.start)
-    for copy, goes, _, _ in first:
-        pl.when(goes)(copy.wait_send)
-    for copy, goes, comes in second:
-        pl.when(goes)(copy.wait_send)
-        pl.when(comes)(copy.wait_recv)
-
-
-def grads_kernel(sizes, factor, pattern, active, q, do, k, v, ld, dqa, dka, dva, pairs, dq, dk, dv):
-    count = list_pairs(sizes, pattern, active, pairs)
+    join_totals(sizes, inbox, dots, ld)
 
     def clear(tile, carried):
         dq[tile] = jnp.zeros(dq.shape[1:], F32)
@@ -365,62 +443,45 @@
         x.reshape(2, tile, feat) for x in (queries, key_tiles, value_tiles, forward_out, out_grad)
     )
     active = tile_active.reshape(-1, tile_active.shape[2])
-    hbm = pl.BlockSpec(memory_space=pl.ANY)
+    hbm = pl.BlockSpec(memory_space=pltpu.HBM)
     vmem = pl.BlockSpec(memory_space=pltpu.VMEM)
     smem = pl.BlockSpec(memory_space=pltpu.SMEM)
     dma = pltpu.SemaphoreType.DMA
 
-    qa, doa, ka, va = pl.pallas_call(
-        functools.partial(gather_kernel, sizes),
+    qa, doa, ka, va, inbox, dots = pl.pallas_call(
+        functools.partial(meet_kernel, sizes, factor),
         out_shape=[
             shape(3, 4, tile, feat),
             shape(3, 4, tile, feat),
             shape(3, 2, tile, feat),
             shape(3, 2, tile, feat),
+            shape(3, 3, 3, 8, tile, dtype=F32),
+            shape(3, 3, 8, tile, dtype=F32),
         ],
-        in_specs=[hbm] * 4,
-        out_specs=[hbm] * 4,
-        scratch_shapes=[dma((4,)), dma((20,)), dma((20,))],
+        in_specs=[smem] * 2 + [hbm] * 5,
+        out_specs=[vmem] * 6,
+        scratch_shapes=[pltpu.VMEM((2, tile, feat), BF16), dma((5,)), dma((52,)), dma((52,))],
         compiler_params=params(0),
-        name="gather",
-    )(q, do, k, v)
+        name="meet",
+    )(pattern, active, q, do, k, v, fo)
     qa, doa = (x.reshape(12, tile, feat) for x in (qa, doa))
     ka, va = (x.reshape(6, tile, feat) for x in (ka, va))
-
-    part = pl.pallas_call(
-        functools.partial(stats_kernel, sizes, factor),
-        out_shape=shape(12, 8, tile, dtype=F32),
-        in_specs=[smem, smem, vmem, vmem, vmem, vmem],
-        out_specs=vmem,
-        scratch_shapes=[pltpu.SMEM((64,), jnp.int32), pltpu.VMEM((13, 8, tile), F32)],
-        compiler_params=params(),
-        name="stats",
-    )(pattern, active, qa, ka, do, fo)
-
-    ld = pl.pallas_call(
-        functools.partial(totals_kernel, sizes),
-        out_shape=shape(3, 4, 8, tile, dtype=F32),
-        in_specs=[vmem],
-        out_specs=vmem,
-        scratch_shapes=[pltpu.VMEM((8, 2, 8, tile), F32), dma((16,)), dma((16,))],
-        compiler_params=params(1),
-        name="totals",
-    )(part.reshape(3, 4, 8, tile))
 
     dqa, dka, dva = pl.pallas_call(
         functools.partial(grads_kernel, sizes, factor),
         out_shape=[shape(12, feat, tile), shape(6, tile, feat), shape(6, tile, feat)],
-        in_specs=[smem, smem, vmem, vmem, vmem, vmem, vmem],
+        in_specs=[smem] * 2 + [vmem] * 6,
         out_specs=[vmem] * 3,
         scratch_shapes=[
             pltpu.SMEM((64,), jnp.int32),
+            pltpu.VMEM((12, 8, tile), F32),
             pltpu.VMEM((13, feat, tile), F32),
             pltpu.VMEM((7, tile, feat), F32),
             pltpu.VMEM((7, tile, feat), F32),
         ],
         compiler_params=params(),
         name="grads",
-    )(pattern, active, qa, doa, ka, va, ld.reshape(12, 8, tile))
+    )(pattern, active, qa, doa, ka, va, inbox, dots)
 
     dq, dk, dv = pl.pallas_call(
         functools.partial(return_kernel, sizes, scale),
@@ -436,7 +497,7 @@
             dma((8,)),
             dma((8,)),
         ],
-        compiler_params=params(2),
+        compiler_params=params(1),
         name="returns",
     )(dqa.reshape(3, 4, feat, tile), dka.reshape(3, 2, tile, feat), dva.reshape(3, 2, tile, feat))
     return dq.reshape(whole), dk.reshape(whole), dv.reshape(whole)

time: 77.5 us -> 68.1 us (0.88)
  Pallas kernels: 68.5 us -> 59.2 us
    pallas_call x3 -> x1, Pallas kernels: 36.2 us -> 28.8 us  [on_device(): pl.pallas_call(functools.partial(meet_kernel, sizes, factor), out_shape=[...]
    pallas_call x1, Pallas kernels: 20.8 us -> 17.4 us  [on_device(): pl.pallas_call(functools.partial(return_kernel, sizes, scale), out_shape=...]
    pallas_call x1, Pallas kernels: 11.5 us -> 13.1 us  [on_device(): pl.pallas_call(functools.partial(grads_kernel, sizes, factor), out_shape=...]
    unnamed x21 -> x17, local copies, waits for them, and re-layouts: 8.03 us -> 8.03 us
where the time goes in v2:
time: 68.1 us; the launch traced here: 67.9 us
  Pallas kernels  59.2 us (87%)
  local copies, waits for them, and re-layouts  8.03 us (12%)
    pallas_call x1, Pallas kernels, on_device(): pl.pallas_call(functools.partial(meet_kernel, sizes, factor), out_shape=[...  28.8 us
    pallas_call x1, Pallas kernels, on_device(): pl.pallas_call(functools.partial(return_kernel, sizes, scale), out_shape=...  17.4 us
    pallas_call x1, Pallas kernels, on_device(): pl.pallas_call(functools.partial(grads_kernel, sizes, factor), out_shape=...  13.1 us
    unnamed x17, local copies, waits for them, and re-layouts  8.03 us

profile of v2, /device:TPU:121, one launch (start us, length us, event | category | flops | bytes accessed | tf_op | source)
XLA Modules:
  0.0 67.9 jit_solution(11040457653681806221)
XLA Ops:
  0.6 0.0 copy-start
  0.6 0.9 %copy-done = bf16[1,1,2,1,384,128]{5,4,3,2,1,0:T(8,128)(2,1)S(1)} copy-done((bf16[1,1,2,1,384,128]{5,4,3,2,1,0:T(8,128)(2,1)S(1)}, bf16[1,1,2,1,384,128]{5,4,3,2,1,0:T(8,128)(2,1)}, u32[]{:S(2)}) %copy-start) | copy-done | bytes 196632
  1.6 0.0 copy-start.1
  1.6 0.9 %copy-done.1 = bf16[1,1,2,1,384,128]{5,4,3,2,1,0:T(8,128)(2,1)S(1)} copy-done((bf16[1,1,2,1,384,128]{5,4,3,2,1,0:T(8,128)(2,1)S(1)}, bf16[1,1,2,1,384,128]{5,4,3,2,1,0:T(8,128)(2,1)}, u32[]{:S(2)}) %copy-start.1) | copy-done | bytes 196632
  2.5 0.0 copy-start.2
  2.5 0.9 %copy-done.2 = bf16[1,1,2,1,384,128]{5,4,3,2,1,0:T(8,128)(2,1)S(1)} copy-done((bf16[1,1,2,1,384,128]{5,4,3,2,1,0:T(8,128)(2,1)S(1)}, bf16[1,1,2,1,384,128]{5,4,3,2,1,0:T(8,128)(2,1)}, u32[]{:S(2)}) %copy-start.2) | copy-done | bytes 196632
  3.4 0.0 copy-start.3
  3.4 0.9 %copy-done.3 = bf16[1,1,2,1,384,128]{5,4,3,2,1,0:T(8,128)(2,1)S(1)} copy-done((bf16[1,1,2,1,384,128]{5,4,3,2,1,0:T(8,128)(2,1)S(1)}, bf16[1,1,2,1,384,128]{5,4,3,2,1,0:T(8,128)(2,1)}, u32[]{:S(2)}) %copy-start.3) | copy-done | bytes 196632
  4.3 0.0 copy-start.4
  4.3 0.9 %copy-done.4 = bf16[1,1,2,1,384,128]{5,4,3,2,1,0:T(8,128)(2,1)S(1)} copy-done((bf16[1,1,2,1,384,128]{5,4,3,2,1,0:T(8,128)(2,1)S(1)}, bf16[1,1,2,1,384,128]{5,4,3,2,1,0:T(8,128)(2,1)}, u32[]{:S(2)}) %copy-start.4) | copy-done | bytes 196632
  5.3 0.0 copy-start.5
  5.3 0.7 %copy-done.5 = s32[4,8,16]{2,1,0:T(8,128)S(1)} copy-done((s32[4,8,16]{2,1,0:T(8,128)S(1)}, s32[4,8,16]{2,1,0:T(8,128)}, u32[]{:S(2)}) %copy-start.5) | copy-done | bytes 2072
  6.0 0.0 copy-start.6
  6.0 0.7 copy-done.6
  6.6 28.8 %meet.1 = (bf16[3,4,384,128]{3,2,1,0:T(8,128)(2,1)S(1)}, bf16[3,4,384,128]{3,2,1,0:T(8,128)(2,1)S(1)}, bf16[3,2,384,128]{3,2,1,0:T(8,128)(2,1)S(1)}, bf16[3,2,38...) custom-call(s32[1,27]{1,0:T(1,128)S(1)} %copy-done.6, ...), custom_call_target="tpu_custom_call" | custom-call | tf_op jit(solution)/shard_map/meet/pallas_call | solution.py:451
  35.4 13.1 %grads.1 = (bf16[12,128,384]{2,1,0:T(8,128)(2,1)S(1)}, bf16[6,384,128]{2,1,0:T(8,128)(2,1)S(1)}, bf16[6,384,128]{2,1,0:T(8,128)(2,1)S(1)}) custom-call(s32[1,27]{1,0:T(1,128)S(1)} %copy-done.6, s32[32,16]{1,0:T(8,128)S(1)} %bitcast.38, bf16[12,384,128]{2,1,0:T(8,128)(2,1)S(1)} %bitcast.23, bf16[12,384,128]{2,1,0:T(8,128)(2,1)S(1)} %bitcast.24, ...), custom_call_target="tpu_custom_call" | custom-call | tf_op jit(solution)/shard_map/grads/pallas_call | solution.py:470
  48.5 17.4 %returns.1 = (bf16[2,384,128]{2,1,0:T(8,128)(2,1)S(1)}, bf16[2,384,128]{2,1,0:T(8,128)(2,1)S(1)}, bf16[2,384,128]{2,1,0:T(8,128)(2,1)S(1)}) custom-call(bf16[3,4,128,384]{3,2,1,0:T(8,128)(2,1)S(1)} %bitcast.22, bf16[3,2,384,128]{3,2,1,0:T(8,128)(2,1)S(1)} %bitcast.25, bf16[3,2,384,128]{3,2,1,0:T(8,128)(2,1)S(1)} %bitcast.26), custom_call_target="tpu_custom_call" | custom-call | tf_op jit(solution)/shard_map/returns/pallas_call | solution.py:486
  65.8 0.7 %copy.16 = bf16[1,1,2,1,384,128]{5,4,3,2,1,0:T(8,128)(2,1)} copy(bf16[1,1,2,1,384,128]{5,4,3,2,1,0:T(8,128)(2,1)S(1)} %bitcast.36) | data formatting | bytes 393216
  66.5 0.7 copy.17
  67.2 0.7 copy.18
Async XLA Ops:
  0.6 0.9 %copy-start = (bf16[1,1,2,1,384,128]{5,4,3,2,1,0:T(8,128)(2,1)S(1)}, bf16[1,1,2,1,384,128]{5,4,3,2,1,0:T(8,128)(2,1)}, u32[]{:S(2)}) copy-start(bf16[1,1,2,1,384,128]{5,4,3,2,1,0:T(8,128)(2,1)} %param.7) | copy-start | bytes 589828
  1.6 0.9 %copy-start.1 = (bf16[1,1,2,1,384,128]{5,4,3,2,1,0:T(8,128)(2,1)S(1)}, bf16[1,1,2,1,384,128]{5,4,3,2,1,0:T(8,128)(2,1)}, u32[]{:S(2)}) copy-start(bf16[1,1,2,1,384,128]{5,4,3,2,1,0:T(8,128)(2,1)} %param.11) | copy-start | bytes 589828
  2.5 0.9 %copy-start.2 = (bf16[1,1,2,1,384,128]{5,4,3,2,1,0:T(8,128)(2,1)S(1)}, bf16[1,1,2,1,384,128]{5,4,3,2,1,0:T(8,128)(2,1)}, u32[]{:S(2)}) copy-start(bf16[1,1,2,1,384,128]{5,4,3,2,1,0:T(8,128)(2,1)} %param.8) | copy-start | bytes 589828
  3.4 0.9 %copy-start.3 = (bf16[1,1,2,1,384,128]{5,4,3,2,1,0:T(8,128)(2,1)S(1)}, bf16[1,1,2,1,384,128]{5,4,3,2,1,0:T(8,128)(2,1)}, u32[]{:S(2)}) copy-start(bf16[1,1,2,1,384,128]{5,4,3,2,1,0:T(8,128)(2,1)} %param.9) | copy-start | bytes 589828
  4.3 0.9 %copy-start.4 = (bf16[1,1,2,1,384,128]{5,4,3,2,1,0:T(8,128)(2,1)S(1)}, bf16[1,1,2,1,384,128]{5,4,3,2,1,0:T(8,128)(2,1)}, u32[]{:S(2)}) copy-start(bf16[1,1,2,1,384,128]{5,4,3,2,1,0:T(8,128)(2,1)} %param.10) | copy-start | bytes 589828
  5.3 0.7 %copy-start.5 = (s32[4,8,16]{2,1,0:T(8,128)S(1)}, s32[4,8,16]{2,1,0:T(8,128)}, u32[]{:S(2)}) copy-start(s32[4,8,16]{2,1,0:T(8,128)} %param.13) | copy-start | bytes 6148
  6.0 0.7 copy-start.6

commit v3 on v2

v3 whole, which is shorter than its diff:
```python
import functools
import math

import jax
import jax.numpy as jnp
from jax import lax
from jax.experimental import pallas as pl
from jax.experimental.pallas import tpu as pltpu
from jax.sharding import PartitionSpec as P

MESH = pl.DeviceIdType.MESH
F32 = jnp.float32
BF16 = jnp.bfloat16
NT = (((1,), (1,)), ((), ()))
TN = (((0,), (0,)), ((), ()))
NN = (((1,), (0,)), ((), ()))
LOW = -1e30


def dot(left, right, form):
    return lax.dot_general(left, right, form, preferred_element_type=F32)


def position():
    return lax.axis_index("ta"), lax.axis_index("ha"), lax.axis_index("wa")


class Links:
    def __init__(self, sizes, send_sem, recv_sem):
        self.sizes = sizes
        self.at = position()
        self.send_sem = send_sem
        self.recv_sem = recv_sem

    def there(self, step):
        found = None
        for place, size, by in zip(self.at, self.sizes, step):
            if by:
                ok = (place + by >= 0) & (place + by < size)
                found = ok if found is None else found & ok
        return found

    def device(self, step):
        return tuple(
            lax.rem(place + by + size, size) for place, size, by in zip(self.at, self.sizes, step)
        )

    def greet(self, steps):
        barrier = pltpu.get_barrier_semaphore()
        count = 0
        for step in steps:
            count = count + self.there(step).astype(jnp.int32)

            @pl.when(self.there(step))
            def _():
                pl.semaphore_signal(
                    barrier, inc=1, device_id=self.device(step), device_id_type=MESH
                )

        pl.semaphore_wait(barrier, count)

    def copy(self, src, dst, number, step):
        return pltpu.make_async_remote_copy(
            src_ref=src,
            dst_ref=dst,
            send_sem=self.send_sem.at[number],
            recv_sem=self.recv_sem.at[number],
            device_id=self.device(step),
            device_id_type=MESH,
        )


def back(step):
    return tuple(-by for by in step)


W_UP, W_DOWN, T_UP, T_DOWN, H_UP, H_DOWN = (
    (0, 0, 1),
    (0, 0, -1),
    (1, 0, 0),
    (-1, 0, 0),
    (0, 1, 0),
    (0, -1, 0),
)


def all_there(*conditions):
    return functools.reduce(jnp.logical_and, conditions)


PLANE = [(dt, dw) for dt in (-1, 0, 1) for dw in (-1, 0, 1) if (dt, dw) != (0, 0)]
WIDE = [(dt, dw) for dt in (-2, -1, 0, 1, 2) for dw in (-1, 0, 1) if (dt, dw) != (0, 0)]


def side_of(dw):
    return dw % 3


PAIRS = [(col, shift) for col in range(2) for shift in range(3)]


def attend_kernel(
    sizes, scale, pattern, active, q, do, k, v, fo, out_dq, out_dk, out_dv,
    qa, doa, ka, va, own_fo, inbox, dots, tops, sums, raised, dq, dk, dv,
    send_q, send_k, send_v, time_in, key_in, value_in, edge, width_in, local_sem, send_sem, recv_sem,
):
    links = Links(sizes, send_sem, recv_sem)
    there = links.there
    t, h, w = links.at
    nt, nh, nw = sizes
    tile = q.shape[1]
    factor = scale * math.log2(math.e)
    row_in = [t > 0, t >= 0, t < nt - 1]
    col_in = [w > 0, w >= 0, w >= 0, w < nw - 1]

    stay = [
        pltpu.make_async_copy(src, dst, local_sem.at[spot])
        for spot, (src, dst) in enumerate(
            (
                (do, doa.at[1, pl.ds(1, 2)]),
                (fo, own_fo),
                (q, qa.at[1, pl.ds(1, 2)]),
                (k, ka.at[1]),
                (v, va.at[1]),
            )
        )
    ]
    for copy in stay:
        copy.start()
    links.greet([(dt, 0, dw) for dt, dw in WIDE] + [H_UP, H_DOWN])

    groups = []
    number = 0
    for rows, rows_all, cols, cols_all in ((q, qa, k, ka), (do, doa, v, va)):
        width = [
            (links.copy(rows.at[1], rows_all.at[1, 0], number, W_UP), there(W_UP), there(W_DOWN)),
            (links.copy(rows.at[0], rows_all.at[1, 3], number + 1, W_DOWN), there(W_DOWN), there(W_UP)),
        ]
        time = [
            (links.copy(rows, rows_all.at[0, pl.ds(1, 2)], number + 2, T_UP), there(T_UP), there(T_DOWN)),
            (links.copy(rows, rows_all.at[2, pl.ds(1, 2)], number + 3, T_DOWN), there(T_DOWN), there(T_UP)),
        ]
        height = [
            (links.copy(cols, cols_all.at[0], number + 4, H_UP), there(H_UP), there(H_DOWN)),
            (links.copy(cols, cols_all.at[2], number + 5, H_DOWN), there(H_DOWN), there(H_UP)),
        ]
        number += 6
        fans = []
        for spot, has in ((0, there(W_DOWN)), (3, there(W_UP))):
            for step, slot in ((T_UP, 0), (T_DOWN, 2)):
                fan = links.copy(rows_all.at[1, spot], rows_all.at[slot, spot], number, step)
                fans.append((fan, has & there(step), has & there(back(step)), slot))
                number += 1
        groups.append((width, time, height, fans))

    def send(group):
        width, time, height, _ = group
        for copy, goes, _ in width + time + height:
            pl.when(goes)(copy.start)

    def arrive(entries):
        for copy, _, comes in entries:
            pl.when(comes)(copy.wait_recv)

    def forward(group):
        width, _, _, fans = group
        arrive(width)
        for fan, goes, _, _ in fans:
            pl.when(goes)(fan.start)

    send(groups[0])
    stay[0].wait()
    stay[1].wait()
    dots[1, 0] = jnp.zeros(dots.shape[2:], F32)
    for spot in range(2):
        both = doa[1, 1 + spot].astype(F32) * own_fo[spot].astype(F32)
        dots[1, 0, spot : spot + 1, :] = jnp.sum(both.T, axis=0, keepdims=True)
    small = []
    for dt, dw in PLANE:
        step = (dt, 0, dw)
        copy = links.copy(dots.at[1, 0], dots.at[1 - dt, side_of(dw)], number, step)
        number += 1
        pl.when(there(step))(copy.start)
        small.append((copy, there(step), there(back(step))))

    def clear(ref, *spot):
        ref[spot] = jnp.zeros(ref.shape[len(spot) :], ref.dtype)

    def clear_sums(x, carried):
        for y in range(4):
            clear(dq, x, y)
        for y in range(2):
            clear(dk, x, y)
            clear(dv, x, y)
        return carried

    lax.fori_loop(0, 3, clear_sums, 0)
    for time in range(3):
        for spot in range(4):
            if (time, spot) not in ((1, 1), (1, 2)):

                @pl.when(jnp.logical_not(row_in[time] & col_in[spot]))
                def _():
                    clear(qa, time, spot)
                    clear(doa, time, spot)

    for row, step in ((0, H_DOWN), (2, H_UP)):

        @pl.when(jnp.logical_not(there(step)))
        def _():
            clear(ka, row)
            clear(va, row)

    def allowed(time, row):
        key_h = h + row - 1
        key_in = (key_h >= 0) & (key_h < nh)
        line = t * nh + jnp.clip(key_h, 0, nh - 1)
        found = []
        for col, shift in PAIRS:
            offset = 9 * (2 - time) + 3 * row + 2 - shift
            on = (active[line, 2 * w + col] == 1) & (pattern[0, offset] == 1)
            inside = key_in & row_in[time] & col_in[col + shift]
            found.append(inside & (on | (offset == 13)))
        return found

    def window(ref, time, col):
        return ref[time, pl.ds(col, 3)].reshape(3 * tile, -1)

    def raise_scores(time, row):
        for col in range(2):
            x = dot(ka[row, col], window(qa, time, col), NT) * factor
            high = jnp.max(x, axis=0, keepdims=True)
            x = jnp.exp2(x - high)
            raised[time, row, col] = x.astype(BF16)
            total = jnp.sum(x, axis=0, keepdims=True)
            for shift in range(3):
                spot = slice(shift * tile, (shift + 1) * tile)
                tops[time, row, 3 * col + shift : 3 * col + shift + 1, :] = high[:, spot]
                sums[time, row, 3 * col + shift : 3 * col + shift + 1, :] = total[:, spot]

    def publish(time):
        nonlocal number
        terms = [[] for _ in range(4)]
        for row in range(3):
            for x, ((col, shift), ok) in enumerate(zip(PAIRS, allowed(time, row))):
                high = jnp.where(ok, tops[time, row, x : x + 1, :], LOW)
                terms[col + shift].append((high, jnp.where(ok, sums[time, row, x : x + 1, :], 0.0)))
        for spot in range(4):
            top = functools.reduce(jnp.maximum, [x for x, _ in terms[spot]])
            inbox[time, time, 0, spot : spot + 1, :] = top
            total = sum(y * jnp.exp2(x - top) for x, y in terms[spot])
            inbox[time, time, 0, 4 + spot : 5 + spot, :] = total
        for dt in (time - 2, time - 1, time):
            for dw in (-1, 0, 1):
                if (dt, dw) == (0, 0):
                    continue
                step = (dt, 0, dw)
                slot = inbox.at[time - dt, time, side_of(dw)]
                copy = links.copy(inbox.at[time, time, 0], slot, number, step)
                number += 1
                goes = row_in[time] & there(step)
                pl.when(goes)(copy.start)
                small.append((copy, goes, row_in[time - dt] & there(back(step))))

    def each(first, last, act):
        def step(x, carried):
            act(x)
            return carried

        lax.fori_loop(first, last, step, 0)

    stay[2].wait()
    stay[3].wait()
    forward(groups[0])
    arrive(groups[0][2])
    send(groups[1])
    each(0, 3, lambda x: raise_scores(1, x))
    publish(1)
    forward(groups[1])
    arrive(groups[0][1])
    arrive([fan[:3] for fan in groups[0][3]])
    each(0, 3, lambda x: raise_scores(0, x))
    publish(0)
    each(0, 3, lambda x: raise_scores(2, x))
    publish(2)
    arrive(groups[1][1] + groups[1][2] + [fan[:3] for fan in groups[1][3]])
    stay[4].wait()
    arrive(small)

    for time in range(3):
        terms = []
        for sender in range(3):
            ok = (t + time - sender >= 0) & (t + time - sender < nt)
            for spot, sides in ((0, (0, 0)), (2, (1, 2))):
                lines = []
                for half, side in enumerate(sides):
                    good = ok if side == 0 else ok & (w > 0) if side == 1 else ok & (w < nw - 1)
                    first = 2 * half if side == 0 else 2 - 2 * half
                    lines.append(
                        (
                            jnp.where(good, inbox[time, sender, side, first : first + 2, :], LOW),
                            jnp.where(good, inbox[time, sender, side, 4 + first : 6 + first, :], 0.0),
                        )
                    )
                terms.append(tuple(jnp.concatenate(x, axis=0) for x in zip(*lines)))
        top = functools.reduce(jnp.maximum, [x for x, _ in terms])
        log_total = top + jnp.log2(sum(y * jnp.exp2(x - top) for x, y in terms))
        for row in range(3):
            for x, ((col, shift), ok) in enumerate(zip(PAIRS, allowed(time, row))):
                part = jnp.exp2(tops[time, row, x : x + 1, :] - log_total[col + shift : col + shift + 1])
                sums[time, row, x : x + 1, :] = jnp.where(ok, part, 0.0)
        for spot, (side, line) in enumerate(((1, 1), (0, 0), (0, 1), (2, 0))):
            part = jnp.where(row_in[time] & col_in[spot], dots[time, side, line : line + 1, :], 0.0)
            for row in range(3):
                tops[time, row, spot : spot + 1, :] = part

    def gradients(time, row):
        for col in range(2):
            rows, slopes = window(qa, time, col), window(doa, time, col)
            weight = jnp.concatenate([sums[time, row, 3 * col + x : 3 * col + x + 1, :] for x in range(3)], axis=1)
            middle = jnp.concatenate([tops[time, row, col + x : col + x + 1, :] for x in range(3)], axis=1)
            probs = raised[time, row, col].astype(F32) * weight
            grads = (probs * (dot(va[row, col], slopes, NT) - middle)).astype(BF16)
            dv[row, col] += dot(probs.astype(BF16), slopes, NN)
            dk[row, col] += dot(grads, rows, NN)
            part = dot(ka[row, col], grads, TN)
            for x in range(3):
                dq[time, col + x] += part[:, x * tile : (x + 1) * tile]

    returns = []
    for src, dst, step in (
        (send_k.at[0], key_in.at[1], H_DOWN),
        (send_v.at[0], value_in.at[1], H_DOWN),
        (send_k.at[1], key_in.at[0], H_UP),
        (send_v.at[1], value_in.at[0], H_UP),
        (send_q.at[0], time_in.at[1], T_DOWN),
        (send_q.at[1], time_in.at[0], T_UP),
        (edge.at[0], width_in.at[1], W_DOWN),
        (edge.at[1], width_in.at[0], W_UP),
    ):
        returns.append((links.copy(src, dst, number, step), there(step), there(back(step)), dst))
        number += 1

    def give(entries):
        for copy, goes, _, _ in entries:
            pl.when(goes)(copy.start)

    def take(entries):
        for copy, _, comes, dst in entries:

            @pl.when(jnp.logical_not(comes))
            def _():
                dst[...] = jnp.zeros(dst.shape, dst.dtype)

            pl.when(comes)(copy.wait_recv)

    for turn, row in ((0, 0), (1, 2)):
        each(0, 3, lambda x: gradients(x, row))
        send_k[turn] = dk[row].astype(BF16)
        send_v[turn] = dv[row].astype(BF16)
        give(returns[2 * turn : 2 * turn + 2])
    each(0, 2, lambda x: gradients(2 * x, 1))
    for turn, time in ((0, 0), (1, 2)):
        send_q[turn] = dq[time].astype(BF16)
    give(returns[4:6])
    gradients(1, 1)
    take(returns[4:6])
    for turn, spot in ((0, 0), (1, 3)):
        total = dq[1, spot] + time_in[0, spot].astype(F32) + time_in[1, spot].astype(F32)
        edge[turn] = total.astype(BF16)
    give(returns[6:8])
    take(returns[0:4])
    for spot in range(2):
        total = dk[1, spot] + key_in[0, spot].astype(F32) + key_in[1, spot].astype(F32)
        out_dk[spot] = (total * scale).astype(BF16)
        total = dv[1, spot] + value_in[0, spot].astype(F32) + value_in[1, spot].astype(F32)
        out_dv[spot] = total.astype(BF16)
    take(returns[6:8])
    for spot in range(2):
        total = dq[1, 1 + spot] + width_in[spot].astype(F32)
        total = total + time_in[0, 1 + spot].astype(F32) + time_in[1, 1 + spot].astype(F32)
        out_dq[spot] = (total * scale).T.astype(BF16)
    for width, time, height, fans in groups:
        for copy, goes, _ in width + time + height + [fan[:3] for fan in fans]:
            pl.when(goes)(copy.wait_send)
    for copy, goes, _ in small + [x[:3] for x in returns]:
        pl.when(goes)(copy.wait_send)


def shape(*dims, dtype=BF16):
    return jax.ShapeDtypeStruct(dims, dtype)


def on_device(sizes, queries, key_tiles, value_tiles, forward_out, out_grad, pattern, tile_active):
    whole = queries.shape
    tile, feat = whole[4], whole[5]
    scale = 1.0 / math.sqrt(feat)
    q, k, v, fo, do = (
        x.reshape(2, tile, feat) for x in (queries, key_tiles, value_tiles, forward_out, out_grad)
    )
    active = tile_active.reshape(-1, tile_active.shape[2])
    hbm = pl.BlockSpec(memory_space=pltpu.HBM)
    vmem = pl.BlockSpec(memory_space=pltpu.VMEM)
    smem = pl.BlockSpec(memory_space=pltpu.SMEM)
    dma = pltpu.SemaphoreType.DMA

    dq, dk, dv = pl.pallas_call(
        functools.partial(attend_kernel, sizes, scale),
        out_shape=[shape(2, tile, feat)] * 3,
        in_specs=[smem] * 2 + [hbm] * 5,
        out_specs=[vmem] * 3,
        scratch_shapes=[
            pltpu.VMEM((3, 4, tile, feat), BF16),
            pltpu.VMEM((3, 4, tile, feat), BF16),
            pltpu.VMEM((3, 2, tile, feat), BF16),
            pltpu.VMEM((3, 2, tile, feat), BF16),
            pltpu.VMEM((2, tile, feat), BF16),
            pltpu.VMEM((3, 3, 3, 8, tile), F32),
            pltpu.VMEM((3, 3, 8, tile), F32),
            pltpu.VMEM((3, 3, 8, tile), F32),
            pltpu.VMEM((3, 3, 8, tile), F32),
            pltpu.VMEM((3, 3, 2, tile, 3 * tile), BF16),
            pltpu.VMEM((3, 4, feat, tile), F32),
            pltpu.VMEM((3, 2, tile, feat), F32),
            pltpu.VMEM((3, 2, tile, feat), F32),
            pltpu.VMEM((2, 4, feat, tile), BF16),
            pltpu.VMEM((2, 2, tile, feat), BF16),
            pltpu.VMEM((2, 2, tile, feat), BF16),
            pltpu.VMEM((2, 4, feat, tile), BF16),
            pltpu.VMEM((2, 2, tile, feat), BF16),
            pltpu.VMEM((2, 2, tile, feat), BF16),
            pltpu.VMEM((2, feat, tile), BF16),
            pltpu.VMEM((2, feat, tile), BF16),
            dma((5,)),
            dma((60,)),
            dma((60,)),
        ],
        compiler_params=pltpu.CompilerParams(
            collective_id=0, has_side_effects=True, vmem_limit_bytes=60 << 20
        ),
        name="attend",
    )(pattern, active, q, do, k, v, fo)
    return dq.reshape(whole), dk.reshape(whole), dv.reshape(whole)


def solution(mesh):
    tiles = P("ta", "ha", "wa", None, None, None)
    sizes = tuple(mesh.shape[axis] for axis in ("ta", "ha", "wa"))
    return jax.shard_map(
        functools.partial(on_device, sizes),
        mesh=mesh,
        in_specs=(tiles,) * 5 + (P(), P()),
        out_specs=(tiles,) * 3,
        check_vma=False,
    )
```

time: 68.1 us -> 68 us (level)
  local copies, waits for them, and re-layouts: 8.03 us -> 3.33 us
  Pallas kernels: 59.2 us -> 63.8 us
    unnamed x17 -> x7, local copies, waits for them, and re-layouts: 8.03 us -> 3.33 us
    pallas_call x3 -> x1, Pallas kernels: 59.2 us -> 63.8 us  [on_device(): pl.pallas_call(functools.partial(attend_kernel, sizes, scale), out_shape=...]
where the time goes in v3:
time: 68 us; the launch traced here: 67.7 us
  Pallas kernels  63.8 us (94%)
  local copies, waits for them, and re-layouts  3.33 us (5%)
    pallas_call x1, Pallas kernels, on_device(): pl.pallas_call(functools.partial(attend_kernel, sizes, scale), out_shape=...  63.8 us
    unnamed x7, local copies, waits for them, and re-layouts  3.33 us

profile of v3, /device:TPU:121, one launch (start us, length us, event | category | flops | bytes accessed | tf_op | source)
XLA Modules:
  0.0 67.7 jit_solution(6219215068072769493)
XLA Ops:
  0.6 63.8 %attend.1 = (bf16[2,384,128]{2,1,0:T(8,128)(2,1)}, bf16[2,384,128]{2,1,0:T(8,128)(2,1)}, bf16[2,384,128]{2,1,0:T(8,128)(2,1)}) custom-call(s32[1,27]{1,0:T(1,128)} %pattern.1, s32[32,16]{1,0:T(8,128)} %bitcast.23, bf16[2,384,128]{2,1,0:T(8,128)(2,1)} %bitcast.15, bf16[2,384,128]{2,1,0:T(8,128)(2,1)} %bitcast.16, bf16[2,384,128]{2,1,0:T(8,128)(2,1)} %bitcast.17, ...), custom_call_target="tpu_custom_call" | custom-call | tf_op jit(solution)/shard_map/attend/pallas_call | solution.py:407
  64.4 0.0 copy-start.1
  64.4 1.7 %copy.16 = bf16[1,1,2,1,384,128]{5,4,3,2,1,0:T(8,128)(2,1)} copy(bf16[1,1,2,1,384,128]{5,4,3,2,1,0:T(8,128)(2,1)} %bitcast.22) | data formatting | bytes 393216
  66.1 0.0 copy-done.1
  66.1 0.0 copy-start
  66.1 0.7 copy.17
  66.7 0.3 copy-done
  67.1 0.7 copy.18
Async XLA Ops:
  64.4 1.7 %copy-start.1 = (bf16[2,384,128]{2,1,0:T(8,128)(2,1)S(1)}, bf16[2,384,128]{2,1,0:T(8,128)(2,1)}, u32[]{:S(2)}) copy-start(bf16[2,384,128]{2,1,0:T(8,128)(2,1)} %get-tuple-element.7) | copy-start | bytes 589828
  66.1 1.0 %copy-start = (bf16[2,384,128]{2,1,0:T(8,128)(2,1)S(1)}, bf16[2,384,128]{2,1,0:T(8,128)(2,1)}, u32[]{:S(2)}) copy-start(bf16[2,384,128]{2,1,0:T(8,128)(2,1)} %get-tuple-element.8) | copy-start | bytes 589828

commit v4 on v3

--- a/solution.py
+++ b/solution.py
@@ -171,7 +171,6 @@
     send(groups[0])
     stay[0].wait()
     stay[1].wait()
-    dots[1, 0] = jnp.zeros(dots.shape[2:], F32)
     for spot in range(2):
         both = doa[1, 1 + spot].astype(F32) * own_fo[spot].astype(F32)
         dots[1, 0, spot : spot + 1, :] = jnp.sum(both.T, axis=0, keepdims=True)
@@ -186,15 +185,13 @@
     def clear(ref, *spot):
         ref[spot] = jnp.zeros(ref.shape[len(spot) :], ref.dtype)
 
-    def clear_sums(x, carried):
+    def clear_sums(x):
         for y in range(4):
             clear(dq, x, y)
         for y in range(2):
             clear(dk, x, y)
             clear(dv, x, y)
-        return carried
-
-    lax.fori_loop(0, 3, clear_sums, 0)
+
     for time in range(3):
         for spot in range(4):
             if (time, spot) not in ((1, 1), (1, 2)):
@@ -226,17 +223,16 @@
     def window(ref, time, col):
         return ref[time, pl.ds(col, 3)].reshape(3 * tile, -1)
 
-    def raise_scores(time, row):
-        for col in range(2):
-            x = dot(ka[row, col], window(qa, time, col), NT) * factor
-            high = jnp.max(x, axis=0, keepdims=True)
-            x = jnp.exp2(x - high)
-            raised[time, row, col] = x.astype(BF16)
-            total = jnp.sum(x, axis=0, keepdims=True)
-            for shift in range(3):
-                spot = slice(shift * tile, (shift + 1) * tile)
-                tops[time, row, 3 * col + shift : 3 * col + shift + 1, :] = high[:, spot]
-                sums[time, row, 3 * col + shift : 3 * col + shift + 1, :] = total[:, spot]
+    def raise_scores(time, row, spots):
+        for col, shift in PAIRS:
+            if col + shift in spots:
+                x = dot(ka[row, col], qa[time, col + shift], NT) * factor
+                high = jnp.max(x, axis=0, keepdims=True)
+                x = jnp.exp2(x - high)
+                raised[time, row, col, :, shift * tile : (shift + 1) * tile] = x.astype(BF16)
+                line = 3 * col + shift
+                tops[time, row, line : line + 1, :] = high
+                sums[time, row, line : line + 1, :] = jnp.sum(x, axis=0, keepdims=True)
 
     def publish(time):
         nonlocal number
@@ -247,16 +243,20 @@
                 terms[col + shift].append((high, jnp.where(ok, sums[time, row, x : x + 1, :], 0.0)))
         for spot in range(4):
             top = functools.reduce(jnp.maximum, [x for x, _ in terms[spot]])
-            inbox[time, time, 0, spot : spot + 1, :] = top
+            half, line = spot // 2, spot % 2
+            inbox[time, time, 0, half, line : line + 1, :] = top
             total = sum(y * jnp.exp2(x - top) for x, y in terms[spot])
-            inbox[time, time, 0, 4 + spot : 5 + spot, :] = total
+            inbox[time, time, 0, half, 2 + line : 3 + line, :] = total
         for dt in (time - 2, time - 1, time):
             for dw in (-1, 0, 1):
                 if (dt, dw) == (0, 0):
                     continue
                 step = (dt, 0, dw)
-                slot = inbox.at[time - dt, time, side_of(dw)]
-                copy = links.copy(inbox.at[time, time, 0], slot, number, step)
+                src, slot = inbox.at[time, time, 0], inbox.at[time - dt, time, 0]
+                if dw:
+                    half = (dw + 1) // 2
+                    src, slot = src.at[half], inbox.at[time - dt, time, 1, 1 - half]
+                copy = links.copy(src, slot, number, step)
                 number += 1
                 goes = row_in[time] & there(step)
                 pl.when(goes)(copy.start)
@@ -269,42 +269,40 @@
 
         lax.fori_loop(first, last, step, 0)
 
+    own, outer = (1, 2), (0, 3)
     stay[2].wait()
     stay[3].wait()
+    raise_scores(1, 1, own)
     forward(groups[0])
     arrive(groups[0][2])
     send(groups[1])
-    each(0, 3, lambda x: raise_scores(1, x))
+    each(0, 2, lambda x: raise_scores(1, 2 * x, own))
+    each(0, 3, lambda x: raise_scores(1, x, outer))
     publish(1)
     forward(groups[1])
     arrive(groups[0][1])
-    arrive([fan[:3] for fan in groups[0][3]])
-    each(0, 3, lambda x: raise_scores(0, x))
-    publish(0)
-    each(0, 3, lambda x: raise_scores(2, x))
-    publish(2)
+    each(0, 6, lambda x: raise_scores(2 * (x // 3), x % 3, own))
+    for time in (0, 2):
+        arrive([fan[:3] for fan in groups[0][3] if fan[3] == time])
+        each(0, 3, lambda x: raise_scores(time, x, outer))
+        publish(time)
+    each(0, 3, clear_sums)
     arrive(groups[1][1] + groups[1][2] + [fan[:3] for fan in groups[1][3]])
     stay[4].wait()
     arrive(small)
 
     for time in range(3):
-        terms = []
-        for sender in range(3):
-            ok = (t + time - sender >= 0) & (t + time - sender < nt)
-            for spot, sides in ((0, (0, 0)), (2, (1, 2))):
-                lines = []
-                for half, side in enumerate(sides):
-                    good = ok if side == 0 else ok & (w > 0) if side == 1 else ok & (w < nw - 1)
-                    first = 2 * half if side == 0 else 2 - 2 * half
-                    lines.append(
-                        (
-                            jnp.where(good, inbox[time, sender, side, first : first + 2, :], LOW),
-                            jnp.where(good, inbox[time, sender, side, 4 + first : 6 + first, :], 0.0),
-                        )
-                    )
-                terms.append(tuple(jnp.concatenate(x, axis=0) for x in zip(*lines)))
-        top = functools.reduce(jnp.maximum, [x for x, _ in terms])
-        log_total = top + jnp.log2(sum(y * jnp.exp2(x - top) for x, y in terms))
+        log_total = []
+        for half, beside in ((0, w > 0), (1, w < nw - 1)):
+            terms = []
+            for sender in range(3):
+                ok = (t + time - sender >= 0) & (t + time - sender < nt)
+                for side, good in ((0, ok), (1, ok & beside)):
+                    both = inbox[time, sender, side, half]
+                    terms.append((jnp.where(good, both[0:2], LOW), jnp.where(good, both[2:4], 0.0)))
+            top = functools.reduce(jnp.maximum, [x for x, _ in terms])
+            log_total.append(top + jnp.log2(sum(y * jnp.exp2(x - top) for x, y in terms)))
+        log_total = jnp.concatenate(log_total, axis=0)
         for row in range(3):
             for x, ((col, shift), ok) in enumerate(zip(PAIRS, allowed(time, row))):
                 part = jnp.exp2(tops[time, row, x : x + 1, :] - log_total[col + shift : col + shift + 1])
@@ -314,8 +312,8 @@
             for row in range(3):
                 tops[time, row, spot : spot + 1, :] = part
 
-    def gradients(time, row):
-        for col in range(2):
+    def gradients(time, row, cols=(0, 1)):
+        for col in cols:
             rows, slopes = window(qa, time, col), window(doa, time, col)
             weight = jnp.concatenate([sums[time, row, 3 * col + x : 3 * col + x + 1, :] for x in range(3)], axis=1)
             middle = jnp.concatenate([tops[time, row, col + x : col + x + 1, :] for x in range(3)], axis=1)
@@ -331,8 +329,10 @@
     for src, dst, step in (
         (send_k.at[0], key_in.at[1], H_DOWN),
         (send_v.at[0], value_in.at[1], H_DOWN),
-        (send_k.at[1], key_in.at[0], H_UP),
-        (send_v.at[1], value_in.at[0], H_UP),
+        (send_k.at[1, 0], key_in.at[0, 0], H_UP),
+        (send_v.at[1, 0], value_in.at[0, 0], H_UP),
+        (send_k.at[1, 1], key_in.at[0, 1], H_UP),
+        (send_v.at[1, 1], value_in.at[0, 1], H_UP),
         (send_q.at[0], time_in.at[1], T_DOWN),
         (send_q.at[1], time_in.at[0], T_UP),
         (edge.at[0], width_in.at[1], W_DOWN),
@@ -354,28 +354,39 @@
 
             pl.when(comes)(copy.wait_recv)
 
-    for turn, row in ((0, 0), (1, 2)):
-        each(0, 3, lambda x: gradients(x, row))
-        send_k[turn] = dk[row].astype(BF16)
-        send_v[turn] = dv[row].astype(BF16)
-        give(returns[2 * turn : 2 * turn + 2])
-    each(0, 2, lambda x: gradients(2 * x, 1))
-    for turn, time in ((0, 0), (1, 2)):
-        send_q[turn] = dq[time].astype(BF16)
-    give(returns[4:6])
+    each(0, 3, lambda x: gradients(2 * x % 3, 0))
+    send_k[0] = dk[0].astype(BF16)
+    send_v[0] = dv[0].astype(BF16)
+    give(returns[0:2])
+
+    def outer_rows(x):
+        gradients(2 * (x // 2), 2 - x % 2)
+        for turn in range(2):
+
+            @pl.when(x == 2 * turn + 1)
+            def _():
+                send_q[turn] = dq[2 * turn].astype(BF16)
+                give(returns[6 + turn : 7 + turn])
+
+    each(0, 4, outer_rows)
+    for col in range(2):
+        gradients(1, 2, (col,))
+        send_k[1, col] = dk[2, col].astype(BF16)
+        send_v[1, col] = dv[2, col].astype(BF16)
+        give(returns[2 + 2 * col : 4 + 2 * col])
     gradients(1, 1)
-    take(returns[4:6])
+    take(returns[6:8])
     for turn, spot in ((0, 0), (1, 3)):
         total = dq[1, spot] + time_in[0, spot].astype(F32) + time_in[1, spot].astype(F32)
         edge[turn] = total.astype(BF16)
-    give(returns[6:8])
-    take(returns[0:4])
+    give(returns[8:10])
+    take(returns[0:6])
     for spot in range(2):
         total = dk[1, spot] + key_in[0, spot].astype(F32) + key_in[1, spot].astype(F32)
         out_dk[spot] = (total * scale).astype(BF16)
         total = dv[1, spot] + value_in[0, spot].astype(F32) + value_in[1, spot].astype(F32)
         out_dv[spot] = total.astype(BF16)
-    take(returns[6:8])
+    take(returns[8:10])
     for spot in range(2):
         total = dq[1, 1 + spot] + width_in[spot].astype(F32)
         total = total + time_in[0, 1 + spot].astype(F32) + time_in[1, 1 + spot].astype(F32)
@@ -385,6 +396,19 @@
             pl.when(goes)(copy.wait_send)
     for copy, goes, _ in small + [x[:3] for x in returns]:
         pl.when(goes)(copy.wait_send)
+
+
+def settle_kernel(*refs):
+    ins, outs, held, sems = refs[:3], refs[3:6], refs[6:9], refs[9]
+    first = [pltpu.make_async_copy(src, dst, sems.at[x]) for x, (src, dst) in enumerate(zip(ins, held))]
+    then = [pltpu.make_async_copy(src, dst, sems.at[3 + x]) for x, (src, dst) in enumerate(zip(held, outs))]
+    for copy in first:
+        copy.start()
+    for one, two in zip(first, then):
+        one.wait()
+        two.start()
+    for copy in then:
+        copy.wait()
 
 
 def shape(*dims, dtype=BF16):
@@ -415,8 +439,8 @@
             pltpu.VMEM((3, 2, tile, feat), BF16),
             pltpu.VMEM((3, 2, tile, feat), BF16),
             pltpu.VMEM((2, tile, feat), BF16),
-            pltpu.VMEM((3, 3, 3, 8, tile), F32),
-            pltpu.VMEM((3, 3, 8, tile), F32),
+            pltpu.VMEM((3, 3, 2, 2, 4, tile), F32),
+            pltpu.VMEM((3, 3, 2, tile), F32),
             pltpu.VMEM((3, 3, 8, tile), F32),
             pltpu.VMEM((3, 3, 8, tile), F32),
             pltpu.VMEM((3, 3, 2, tile, 3 * tile), BF16),
@@ -432,14 +456,23 @@
             pltpu.VMEM((2, feat, tile), BF16),
             pltpu.VMEM((2, feat, tile), BF16),
             dma((5,)),
-            dma((60,)),
-            dma((60,)),
+            dma((62,)),
+            dma((62,)),
         ],
         compiler_params=pltpu.CompilerParams(
             collective_id=0, has_side_effects=True, vmem_limit_bytes=60 << 20
         ),
         name="attend",
     )(pattern, active, q, do, k, v, fo)
+    dq, dk, dv = pl.pallas_call(
+        settle_kernel,
+        out_shape=[shape(2, tile, feat)] * 3,
+        in_specs=[hbm] * 3,
+        out_specs=[hbm] * 3,
+        scratch_shapes=[pltpu.VMEM((2, tile, feat), BF16)] * 3 + [dma((6,))],
+        compiler_params=pltpu.CompilerParams(vmem_limit_bytes=60 << 20),
+        name="settle",
+    )(dq, dk, dv)
     return dq.reshape(whole), dk.reshape(whole), dv.reshape(whole)
 
 

time: 68 us -> 64.2 us (0.944)
  the two profiles are of different devices: /device:TPU:121 before, /device:TPU:102 now
where the time goes in v4:
time: 64.2 us; the launch traced here: 64 us
  Pallas kernels  63.4 us (99%)
    pallas_call x1, Pallas kernels, on_device(): pl.pallas_call(functools.partial(attend_kernel, sizes, scale), out_shape=...  61.5 us
    pallas_call x1, Pallas kernels, on_device(): pl.pallas_call(settle_kernel, out_shape=[shape(2, tile, feat)] * 3, in_sp...  1.84 us

profile of v4, /device:TPU:102, one launch (start us, length us, event | category | flops | bytes accessed | tf_op | source)
XLA Modules:
  0.0 64.0 jit_solution(15818434631164482521)
XLA Ops:
  0.6 61.5 %attend.1 = (bf16[2,384,128]{2,1,0:T(8,128)(2,1)}, bf16[2,384,128]{2,1,0:T(8,128)(2,1)}, bf16[2,384,128]{2,1,0:T(8,128)(2,1)}) custom-call(s32[1,27]{1,0:T(1,128)} %pattern.1, s32[32,16]{1,0:T(8,128)} %bitcast.20, bf16[2,384,128]{2,1,0:T(8,128)(2,1)} %bitcast.15, bf16[2,384,128]{2,1,0:T(8,128)(2,1)} %bitcast.16, bf16[2,384,128]{2,1,0:T(8,128)(2,1)} %bitcast.17, ...), custom_call_target="tpu_custom_call" | custom-call | tf_op jit(solution)/shard_map/attend/pallas_call | solution.py:431
  62.2 1.8 %settle.1 = (bf16[2,384,128]{2,1,0:T(8,128)(2,1)}, bf16[2,384,128]{2,1,0:T(8,128)(2,1)}, bf16[2,384,128]{2,1,0:T(8,128)(2,1)}) custom-call(bf16[2,384,128]{2,1,0:T(8,128)(2,1)} %get-tuple-element.9.refs_0_, bf16[2,384,128]{2,1,0:T(8,128)(2,1)} %get-tuple-element.10.refs_1_, bf16[2,384,128]{2,1,0:T(8,128)(2,1)} %get-tuple-element.11.refs_2_), custom_call_target="tpu_custom_call" | custom-call | tf_op jit(solution)/shard_map/settle/pallas_call | solution.py:467

commit v5 on v4

--- a/solution.py
+++ b/solution.py
@@ -102,7 +102,7 @@
 def attend_kernel(
     sizes, scale, pattern, active, q, do, k, v, fo, out_dq, out_dk, out_dv,
     qa, doa, ka, va, own_fo, inbox, dots, tops, sums, raised, dq, dk, dv,
-    send_q, send_k, send_v, time_in, key_in, value_in, edge, width_in, local_sem, send_sem, recv_sem,
+    send_q, send_k, send_v, time_in, corner_in, key_in, value_in, edge, width_in, local_sem, send_sem, recv_sem,
 ):
     links = Links(sizes, send_sem, recv_sem)
     there = links.there
@@ -153,9 +153,8 @@
                 number += 1
         groups.append((width, time, height, fans))
 
-    def send(group):
-        width, time, height, _ = group
-        for copy, goes, _ in width + time + height:
+    def send(entries):
+        for copy, goes, _ in entries:
             pl.when(goes)(copy.start)
 
     def arrive(entries):
@@ -168,7 +167,7 @@
         for fan, goes, _, _ in fans:
             pl.when(goes)(fan.start)
 
-    send(groups[0])
+    send(groups[0][0] + groups[0][1] + groups[0][2] + groups[1][0])
     stay[0].wait()
     stay[1].wait()
     for spot in range(2):
@@ -220,19 +219,16 @@
             found.append(inside & (on | (offset == 13)))
         return found
 
-    def window(ref, time, col):
-        return ref[time, pl.ds(col, 3)].reshape(3 * tile, -1)
-
-    def raise_scores(time, row, spots):
-        for col, shift in PAIRS:
-            if col + shift in spots:
-                x = dot(ka[row, col], qa[time, col + shift], NT) * factor
-                high = jnp.max(x, axis=0, keepdims=True)
-                x = jnp.exp2(x - high)
-                raised[time, row, col, :, shift * tile : (shift + 1) * tile] = x.astype(BF16)
-                line = 3 * col + shift
-                tops[time, row, line : line + 1, :] = high
-                sums[time, row, line : line + 1, :] = jnp.sum(x, axis=0, keepdims=True)
+    def raise_scores(time, rows, spots):
+        taken = [(row, col, shift) for row in rows for col, shift in PAIRS if col + shift in spots]
+        scores = [dot(ka[row, col], qa[time, col + shift], NT) * factor for row, col, shift in taken]
+        highs = [jnp.max(x, axis=0, keepdims=True) for x in scores]
+        for (row, col, shift), x, high in zip(taken, scores, highs):
+            x = jnp.exp2(x - high)
+            raised[time, row, col, :, shift * tile : (shift + 1) * tile] = x.astype(BF16)
+            line = 3 * col + shift
+            tops[time, row, line : line + 1, :] = high
+            sums[time, row, line : line + 1, :] = jnp.sum(x, axis=0, keepdims=True)
 
     def publish(time):
         nonlocal number
@@ -272,19 +268,19 @@
     own, outer = (1, 2), (0, 3)
     stay[2].wait()
     stay[3].wait()
-    raise_scores(1, 1, own)
+    raise_scores(1, (1,), own)
     forward(groups[0])
     arrive(groups[0][2])
-    send(groups[1])
-    each(0, 2, lambda x: raise_scores(1, 2 * x, own))
-    each(0, 3, lambda x: raise_scores(1, x, outer))
+    send(groups[1][1] + groups[1][2])
+    raise_scores(1, (0, 2), own)
+    raise_scores(1, (0, 1, 2), outer)
     publish(1)
     forward(groups[1])
     arrive(groups[0][1])
-    each(0, 6, lambda x: raise_scores(2 * (x // 3), x % 3, own))
+    each(0, 2, lambda x: raise_scores(2 * x, (0, 1, 2), own))
     for time in (0, 2):
         arrive([fan[:3] for fan in groups[0][3] if fan[3] == time])
-        each(0, 3, lambda x: raise_scores(time, x, outer))
+        raise_scores(time, (0, 1, 2), outer)
         publish(time)
     each(0, 3, clear_sums)
     arrive(groups[1][1] + groups[1][2] + [fan[:3] for fan in groups[1][3]])
@@ -312,18 +308,20 @@
             for row in range(3):
                 tops[time, row, spot : spot + 1, :] = part
 
-    def gradients(time, row, cols=(0, 1)):
-        for col in cols:
-            rows, slopes = window(qa, time, col), window(doa, time, col)
-            weight = jnp.concatenate([sums[time, row, 3 * col + x : 3 * col + x + 1, :] for x in range(3)], axis=1)
-            middle = jnp.concatenate([tops[time, row, col + x : col + x + 1, :] for x in range(3)], axis=1)
-            probs = raised[time, row, col].astype(F32) * weight
+    def gradients(time, row, parts=((0, 0, 3), (1, 0, 3))):
+        for col, first, many in parts:
+            begin, shifts = col + first, range(first, first + many)
+            rows = qa[time, begin : begin + many].reshape(many * tile, -1)
+            slopes = doa[time, begin : begin + many].reshape(many * tile, -1)
+            weight = jnp.concatenate([sums[time, row, 3 * col + x : 3 * col + x + 1, :] for x in shifts], axis=1)
+            middle = jnp.concatenate([tops[time, row, col + x : col + x + 1, :] for x in shifts], axis=1)
+            probs = raised[time, row, col, :, first * tile : (first + many) * tile].astype(F32) * weight
             grads = (probs * (dot(va[row, col], slopes, NT) - middle)).astype(BF16)
             dv[row, col] += dot(probs.astype(BF16), slopes, NN)
             dk[row, col] += dot(grads, rows, NN)
             part = dot(ka[row, col], grads, TN)
-            for x in range(3):
-                dq[time, col + x] += part[:, x * tile : (x + 1) * tile]
+            for x in range(many):
+                dq[time, begin + x] += part[:, x * tile : (x + 1) * tile]
 
     returns = []
     for src, dst, step in (
@@ -333,8 +331,12 @@
         (send_v.at[1, 0], value_in.at[0, 0], H_UP),
         (send_k.at[1, 1], key_in.at[0, 1], H_UP),
         (send_v.at[1, 1], value_in.at[0, 1], H_UP),
-        (send_q.at[0], time_in.at[1], T_DOWN),
-        (send_q.at[1], time_in.at[0], T_UP),
+        (send_q.at[0, pl.ds(1, 2)], time_in.at[1], T_DOWN),
+        (send_q.at[0, 0], corner_in.at[1, 1], (-1, 0, -1)),
+        (send_q.at[0, 3], corner_in.at[1, 0], (-1, 0, 1)),
+        (send_q.at[1, pl.ds(1, 2)], time_in.at[0], T_UP),
+        (send_q.at[1, 0], corner_in.at[0, 1], (1, 0, -1)),
+        (send_q.at[1, 3], corner_in.at[0, 0], (1, 0, 1)),
         (edge.at[0], width_in.at[1], W_DOWN),
         (edge.at[1], width_in.at[0], W_UP),
     ):
@@ -359,37 +361,36 @@
     send_v[0] = dv[0].astype(BF16)
     give(returns[0:2])
 
-    def outer_rows(x):
-        gradients(2 * (x // 2), 2 - x % 2)
-        for turn in range(2):
-
-            @pl.when(x == 2 * turn + 1)
-            def _():
-                send_q[turn] = dq[2 * turn].astype(BF16)
-                give(returns[6 + turn : 7 + turn])
-
-    each(0, 4, outer_rows)
+    def hand_over(turn):
+        send_q[turn] = dq[2 * turn].astype(BF16)
+        give(returns[6 + 3 * turn : 9 + 3 * turn])
+
+    each(0, 2, lambda x: gradients(0, 2 - x))
+    hand_over(0)
+    gradients(2, 2)
     for col in range(2):
-        gradients(1, 2, (col,))
+        gradients(1, 2, ((col, 0, 3),))
         send_k[1, col] = dk[2, col].astype(BF16)
         send_v[1, col] = dv[2, col].astype(BF16)
         give(returns[2 + 2 * col : 4 + 2 * col])
-    gradients(1, 1)
-    take(returns[6:8])
+    gradients(2, 1)
+    hand_over(1)
+    gradients(1, 1, ((0, 0, 1), (1, 2, 1)))
     for turn, spot in ((0, 0), (1, 3)):
-        total = dq[1, spot] + time_in[0, spot].astype(F32) + time_in[1, spot].astype(F32)
-        edge[turn] = total.astype(BF16)
-    give(returns[8:10])
+        edge[turn] = dq[1, spot].astype(BF16)
+    give(returns[12:14])
+    gradients(1, 1, ((0, 1, 2), (1, 0, 2)))
     take(returns[0:6])
     for spot in range(2):
         total = dk[1, spot] + key_in[0, spot].astype(F32) + key_in[1, spot].astype(F32)
         out_dk[spot] = (total * scale).astype(BF16)
         total = dv[1, spot] + value_in[0, spot].astype(F32) + value_in[1, spot].astype(F32)
         out_dv[spot] = total.astype(BF16)
-    take(returns[8:10])
+    take(returns[6:14])
     for spot in range(2):
         total = dq[1, 1 + spot] + width_in[spot].astype(F32)
-        total = total + time_in[0, 1 + spot].astype(F32) + time_in[1, 1 + spot].astype(F32)
+        for turn in range(2):
+            total = total + time_in[turn, spot].astype(F32) + corner_in[turn, spot].astype(F32)
         out_dq[spot] = (total * scale).T.astype(BF16)
     for width, time, height, fans in groups:
         for copy, goes, _ in width + time + height + [fan[:3] for fan in fans]:
@@ -450,14 +451,15 @@
             pltpu.VMEM((2, 4, feat, tile), BF16),
             pltpu.VMEM((2, 2, tile, feat), BF16),
             pltpu.VMEM((2, 2, tile, feat), BF16),
-            pltpu.VMEM((2, 4, feat, tile), BF16),
+            pltpu.VMEM((2, 2, feat, tile), BF16),
+            pltpu.VMEM((2, 2, feat, tile), BF16),
             pltpu.VMEM((2, 2, tile, feat), BF16),
             pltpu.VMEM((2, 2, tile, feat), BF16),
             pltpu.VMEM((2, feat, tile), BF16),
             pltpu.VMEM((2, feat, tile), BF16),
             dma((5,)),
-            dma((62,)),
-            dma((62,)),
+            dma((66,)),
+            dma((66,)),
         ],
         compiler_params=pltpu.CompilerParams(
             collective_id=0, has_side_effects=True, vmem_limit_bytes=60 << 20

time: 64.2 us -> 58.8 us (0.916)
  the two profiles are of different devices: /device:TPU:102 before, /device:TPU:121 now
where the time goes in v5:
time: 58.8 us; the launch traced here: 58.4 us
  Pallas kernels  57.6 us (98%)
  between operations  0.8 us (1%)
    pallas_call x1, Pallas kernels, on_device(): pl.pallas_call(functools.partial(attend_kernel, sizes, scale), out_shape=...  55.7 us
    pallas_call x1, Pallas kernels, on_device(): pl.pallas_call(settle_kernel, out_shape=[shape(2, tile, feat)] * 3, in_sp...  1.84 us

profile of v5, /device:TPU:121, one launch (start us, length us, event | category | flops | bytes accessed | tf_op | source)
XLA Modules:
  0.0 58.4 jit_solution(5222623662653948073)
XLA Ops:
  0.6 55.7 %attend.1 = (bf16[2,384,128]{2,1,0:T(8,128)(2,1)}, bf16[2,384,128]{2,1,0:T(8,128)(2,1)}, bf16[2,384,128]{2,1,0:T(8,128)(2,1)}) custom-call(s32[1,27]{1,0:T(1,128)} %pattern.1, s32[32,16]{1,0:T(8,128)} %bitcast.20, bf16[2,384,128]{2,1,0:T(8,128)(2,1)} %bitcast.15, bf16[2,384,128]{2,1,0:T(8,128)(2,1)} %bitcast.16, bf16[2,384,128]{2,1,0:T(8,128)(2,1)} %bitcast.17, ...), custom_call_target="tpu_custom_call" | custom-call | tf_op jit(solution)/shard_map/attend/pallas_call | solution.py:432
  56.3 1.8 %settle.1 = (bf16[2,384,128]{2,1,0:T(8,128)(2,1)}, bf16[2,384,128]{2,1,0:T(8,128)(2,1)}, bf16[2,384,128]{2,1,0:T(8,128)(2,1)}) custom-call(bf16[2,384,128]{2,1,0:T(8,128)(2,1)} %get-tuple-element.9.refs_0_, bf16[2,384,128]{2,1,0:T(8,128)(2,1)} %get-tuple-element.10.refs_1_, bf16[2,384,128]{2,1,0:T(8,128)(2,1)} %get-tuple-element.11.refs_2_), custom_call_target="tpu_custom_call" | custom-call | tf_op jit(solution)/shard_map/settle/pallas_call | solution.py:469

commit v6 on v5

--- a/solution.py
+++ b/solution.py
@@ -230,19 +230,30 @@
             tops[time, row, line : line + 1, :] = high
             sums[time, row, line : line + 1, :] = jnp.sum(x, axis=0, keepdims=True)
 
+    def mask(time, row):
+        lines = [jnp.full((1, tile), ok.astype(jnp.int32)) for ok in allowed(time, row)]
+        return jnp.concatenate(lines, axis=0) == 1
+
+    def by_spot(six, join):
+        return jnp.concatenate([six[0:1], join(six[1:3], six[3:5]), six[5:6]], axis=0)
+
+    def by_pair(four):
+        return jnp.concatenate([four[0:3], four[1:4]], axis=0)
+
     def publish(time):
         nonlocal number
-        terms = [[] for _ in range(4)]
+        highs = []
         for row in range(3):
-            for x, ((col, shift), ok) in enumerate(zip(PAIRS, allowed(time, row))):
-                high = jnp.where(ok, tops[time, row, x : x + 1, :], LOW)
-                terms[col + shift].append((high, jnp.where(ok, sums[time, row, x : x + 1, :], 0.0)))
-        for spot in range(4):
-            top = functools.reduce(jnp.maximum, [x for x, _ in terms[spot]])
-            half, line = spot // 2, spot % 2
-            inbox[time, time, 0, half, line : line + 1, :] = top
-            total = sum(y * jnp.exp2(x - top) for x, y in terms[spot])
-            inbox[time, time, 0, half, 2 + line : 3 + line, :] = total
+            highs.append(jnp.where(mask(time, row), tops[time, row, 0:6, :], LOW))
+        top = by_spot(functools.reduce(jnp.maximum, highs), jnp.maximum)
+        total = 0.0
+        for row in range(3):
+            part = jnp.exp2(highs[row] - by_pair(top)) * sums[time, row, 0:6, :]
+            total = total + jnp.where(mask(time, row), part, 0.0)
+        total = by_spot(total, jnp.add)
+        for half in range(2):
+            inbox[time, time, 0, half, 0:2, :] = top[2 * half : 2 * half + 2]
+            inbox[time, time, 0, half, 2:4, :] = total[2 * half : 2 * half + 2]
         for dt in (time - 2, time - 1, time):
             for dw in (-1, 0, 1):
                 if (dt, dw) == (0, 0):
@@ -269,10 +280,11 @@
     stay[2].wait()
     stay[3].wait()
     raise_scores(1, (1,), own)
+    arrive(groups[0][2])
+    send(groups[1][2])
+    raise_scores(1, (0, 2), own)
     forward(groups[0])
-    arrive(groups[0][2])
-    send(groups[1][1] + groups[1][2])
-    raise_scores(1, (0, 2), own)
+    send(groups[1][1])
     raise_scores(1, (0, 1, 2), outer)
     publish(1)
     forward(groups[1])
@@ -300,9 +312,8 @@
             log_total.append(top + jnp.log2(sum(y * jnp.exp2(x - top) for x, y in terms)))
         log_total = jnp.concatenate(log_total, axis=0)
         for row in range(3):
-            for x, ((col, shift), ok) in enumerate(zip(PAIRS, allowed(time, row))):
-                part = jnp.exp2(tops[time, row, x : x + 1, :] - log_total[col + shift : col + shift + 1])
-                sums[time, row, x : x + 1, :] = jnp.where(ok, part, 0.0)
+            part = jnp.exp2(tops[time, row, 0:6, :] - by_pair(log_total))
+            sums[time, row, 0:6, :] = jnp.where(mask(time, row), part, 0.0)
         for spot, (side, line) in enumerate(((1, 1), (0, 0), (0, 1), (2, 0))):
             part = jnp.where(row_in[time] & col_in[spot], dots[time, side, line : line + 1, :], 0.0)
             for row in range(3):

time: 58.8 us -> 58.9 us (level)
  no operation moved by 1% of the time
where the time goes in v6:
time: 58.9 us; the launch traced here: 58.4 us
  Pallas kernels  57.6 us (98%)
  between operations  0.8 us (1%)
    pallas_call x1, Pallas kernels, on_device(): pl.pallas_call(functools.partial(attend_kernel, sizes, scale), out_shape=...  55.8 us
    pallas_call x1, Pallas kernels, on_device(): pl.pallas_call(settle_kernel, out_shape=[shape(2, tile, feat)] * 3, in_sp...  1.84 us

profile of v6, /device:TPU:121, one launch (start us, length us, event | category | flops | bytes accessed | tf_op | source)
XLA Modules:
  0.0 58.4 jit_solution(7297765655715516041)
XLA Ops:
  0.6 55.8 %attend.1 = (bf16[2,384,128]{2,1,0:T(8,128)(2,1)}, bf16[2,384,128]{2,1,0:T(8,128)(2,1)}, bf16[2,384,128]{2,1,0:T(8,128)(2,1)}) custom-call(s32[1,27]{1,0:T(1,128)} %pattern.1, s32[32,16]{1,0:T(8,128)} %bitcast.20, bf16[2,384,128]{2,1,0:T(8,128)(2,1)} %bitcast.15, bf16[2,384,128]{2,1,0:T(8,128)(2,1)} %bitcast.16, bf16[2,384,128]{2,1,0:T(8,128)(2,1)} %bitcast.17, ...), custom_call_target="tpu_custom_call" | custom-call | tf_op jit(solution)/shard_map/attend/pallas_call | solution.py:443
  56.4 1.8 %settle.1 = (bf16[2,384,128]{2,1,0:T(8,128)(2,1)}, bf16[2,384,128]{2,1,0:T(8,128)(2,1)}, bf16[2,384,128]{2,1,0:T(8,128)(2,1)}) custom-call(bf16[2,384,128]{2,1,0:T(8,128)(2,1)} %get-tuple-element.9.refs_0_, bf16[2,384,128]{2,1,0:T(8,128)(2,1)} %get-tuple-element.10.refs_1_, bf16[2,384,128]{2,1,0:T(8,128)(2,1)} %get-tuple-element.11.refs_2_), custom_call_target="tpu_custom_call" | custom-call | tf_op jit(solution)/shard_map/settle/pallas_call | solution.py:480
